TPU v7x, 256 devices: a whole 4x4x8 slice. The times are simulated.
256 devices in a mesh: context: 32 (over y, z), tensor: 8 (over x, core).
Axes of the slice: x: 4, y: 4, z: 8, core: 2. Of those that a mesh axis runs over, the one named last changes fastest.
Arguments:
- stream_rows: bfloat16 [9216, 7168], P('context', 'tensor'), may hold values from -3 to 3
- picks: int32 [9216], P('context'), may hold values from 0 to 1536, as said below
- router: float32 [9216], P('context'), may hold values from 0.25 to 2
- queries: bfloat16 [9216, 4096], P('context', 'tensor'), may hold values from -100 to 100
- keys: bfloat16 [9216, 1024], P('context', 'tensor'), may hold values from -6 to 6
- values: bfloat16 [9216, 1024], P('context', 'tensor'), may hold values from -6 to 6
- out_weight: bfloat16 [4096, 7168], P('tensor'), may hold values from -0.09375 to 0.09375
Outputs:
- updated: bfloat16 [9216, 7168], P('context', 'tensor')
Inputs may be any that keep to these rules, and one draw needn't show every extreme that they name: `picks`: each block of 288 slots (one index of context) holds distinct local token indices in increasing order followed by entries equal to 1536; a block has 96 to 288 picked tokens, and some block has exactly 288.
All inputs are finite; a program needn't handle non-finite values.
Results may differ from a plain program's by a relative error of at most 0.012.
Values may be sent and summed in bfloat16 or wider, within the bound.
A program may use at most 64 MiB of HBM per device.

v0:
```python
import math

import jax
import jax.numpy as jnp
from jax import lax
from jax.sharding import PartitionSpec as P

HD = 128
TOK_DEV = 1536


NEG_FILL = -1e30


def online_step(
    softmax_state, query_block, query_pos, key_block, value_block, key_pos, score_scale
):
    row_max, row_total, mixed_out = softmax_state
    scores = (
        jnp.einsum("qkgd,skd->kgqs", query_block, key_block, preferred_element_type=jnp.float32)
        * score_scale
    )
    visible = key_pos[None, :] <= query_pos[:, None]
    scores = jnp.where(visible[None, None], scores, NEG_FILL)
    new_max = jnp.maximum(row_max, jnp.max(scores, axis=-1))
    factor = jnp.exp(row_max - new_max)
    weights = jnp.exp(scores - new_max[..., None])
    row_total = factor * row_total + jnp.sum(weights, axis=-1)
    increment = jnp.einsum(
        "kgqs,skd->qkgd",
        weights.astype(jnp.bfloat16),
        value_block,
        preferred_element_type=jnp.float32,
    )
    mixed_out = mixed_out * jnp.transpose(factor, (2, 0, 1))[..., None] + increment
    return (new_max, row_total, mixed_out)


def fresh_state(row_count, kv_local, group_size, head_dim):
    return (
        jnp.full((kv_local, group_size, row_count), NEG_FILL, jnp.float32),
        jnp.zeros((kv_local, group_size, row_count), jnp.float32),
        jnp.zeros((row_count, kv_local, group_size, head_dim), jnp.float32),
    )


def finish_state(softmax_state):
    row_max, row_total, mixed_out = softmax_state
    totals = jnp.transpose(row_total, (2, 0, 1))[..., None]
    result = jnp.where(totals > 0, mixed_out / jnp.where(totals > 0, totals, 1.0), 0.0)
    return result.reshape(result.shape[0], -1).astype(jnp.bfloat16)


def local(stream_rows, picks, router, queries, keys, values, out_weight):
    slot_count = picks.shape[0]
    context_size = lax.axis_size("context")
    context_index = lax.axis_index("context")
    token_total = TOK_DEV * context_size
    is_valid = picks < TOK_DEV
    global_pos = context_index * TOK_DEV + picks
    key_pos = jnp.where(is_valid, global_pos, token_total)
    query_pos = jnp.where(is_valid, global_pos, -1)
    head_dim = HD
    kv_local = keys.shape[1] // head_dim
    head_local = queries.shape[1] // head_dim
    group_size = head_local // kv_local
    score_scale = head_dim ** (-0.5)
    query_grid = queries.reshape(slot_count, kv_local, group_size, head_dim)
    query_sets = [(query_grid, query_pos)]
    initial = tuple(
        (fresh_state(item[1].shape[0], kv_local, group_size, head_dim) for item in query_sets)
    )
    running = initial
    key_piece = lax.all_gather(keys, "context", axis=0, tiled=True)
    value_piece = lax.all_gather(values, "context", axis=0, tiled=True)
    pos_piece = lax.all_gather(key_pos, "context", axis=0, tiled=True)
    shards_here = key_piece.shape[0] // slot_count
    per_step = math.gcd(shards_here, 4) * slot_count
    blocks = key_piece.shape[0] // per_step
    key_split = key_piece.reshape(blocks, per_step, kv_local, head_dim)
    value_split = value_piece.reshape(blocks, per_step, kv_local, head_dim)
    pos_split = pos_piece.reshape(blocks, per_step)

    def one_block(states, block_items):
        key_block, value_block, block_pos = block_items
        query_block, set_pos = query_sets[0]

        def apply_step(current, query_block=query_block, set_pos=set_pos):
            return online_step(
                current, query_block, set_pos, key_block, value_block, block_pos, score_scale
            )

        updated_states = [apply_step(states[0])]
        return (tuple(updated_states), None)

    running, _ = lax.scan(one_block, running, (key_split, value_split, pos_split))
    attended = finish_state(running[0])
    scattered = lax.psum_scatter(
        lax.dot_general(
            out_weight, attended, (((0,), (1,)), ((), ())), preferred_element_type=jnp.float32
        ).astype(jnp.bfloat16),
        "tensor",
        scatter_dimension=0,
        tiled=True,
    ).astype(jnp.float32)
    projected = jnp.transpose(scattered)
    residual = stream_rows.astype(jnp.float32)
    updated = jnp.where(is_valid[:, None], residual + router[:, None] * projected, residual)
    return updated.astype(jnp.bfloat16)


def solution(mesh):
    placed = (
        P("context", "tensor"),
        P("context"),
        P("context"),
        P("context", "tensor"),
        P("context", "tensor"),
        P("context", "tensor"),
        P("tensor", None),
    )
    return jax.shard_map(
        local, mesh=mesh, in_specs=placed, out_specs=P("context", "tensor"), check_vma=False
    )
```

profile of v0, /device:TPU:25, one launch (start us, length us, event | category | flops | bytes accessed | tf_op | source)
XLA Modules:
  0.0 313.6 jit_solution(13185876721474340337)
XLA Ops:
  6.5 0.7 all-gather.3.cloned.1.call-update
  7.3 0.7 all-gather.5.cloned.1.call-update
  8.1 1.3 dynamic-slice
  10.1 0.8 add_select_fusion.1
  10.8 105.5 %all-reduce = s32[9216]{0:T(1024)S(1)} all-reduce(s32[9216]{0:T(1024)S(1)} %get-tuple-element.126), channel_id=1, replica_groups=mesh['context'=32,'tensor'=8] {'context'}, use_global_device_ids=true, to_apply=%add | all-reduce | flops 9216 | bytes 73728
  116.3 1.0 reshape.95
  117.4 47.1 %all-gather.5.cloned.1.call-done = bf16[9216,128]{1,0:T(8,128)(2,1)} async-done(((bf16[288,128]{1,0:T(8,128)(2,1)}), bf16[9216,128]{1,0:T(8,128)(2,1)}) %all-gather.5.cloned.1.call-update) | async-done | bytes 2359312 | tf_op jit(solution)/shard_map/all_gather | solution.py:75
  164.6 81.5 %while.15 = (s32[]{:T(128)}, f32[1,4,288]{2,1,0:T(4,128)S(1)}, f32[1,4,288]{2,1,0:T(4,128)S(1)}, f32[288,1,4,128]{3,0,2,1:T(8,128)S(1)}, s32[8,1152]{1,0:T(8,128...) while((s32[]{:T(128)}, f32[1,4,288]{2,1,0:T(4,128)S(1)}, ...), condition=%wide.region_3.4_spmd.clone, body=%wide.region_0.3_spmd.clone.sunk | while | flops 689548032 | bytes 39976728 | solution.py:96
  164.6 0.3 broadcast_compare_fusion.3
  164.8 4.5 %fusion.34 = (f32[4,288]{1,0:T(4,128)S(1)}, f32[1,4,288,1152]{3,2,1,0:T(8,128)}) fusion(bf16[288,1,4,128]{3,0,2,1:T(8,128)(2,1)S(1)} %get-tuple-element.219, bf16[8,1152,1,128]{3,1,2,0:T(8,128)(2,1)} %get-tuple-element.218, s32[]{:T(128)} %get-tuple-element.201, pred[288,1152]{1,0:T(8,128)(4,1)S(1)} %broadcast_compare_fusion.3), kind=kOutput, calls=%fused_computation.36.clone.1 | convolution fusion | flops 343718784 | bytes 6235136 | tf_op jit(solution)/shard_map/while/body/eval_jaxpr/qkgd,skd->kgqs/dot_general | solution.py:20
  169.4 4.0 %fusion.37 = f32[288,1,4,128]{3,0,2,1:T(8,128)S(1)} fusion(f32[1,4,288,1152]{3,2,1,0:T(8,128)} %get-tuple-element.188, f32[4,288]{1,0:T(4,128)S(1)} %bitcast.82, f32[288,1,4,128]{3,0,2,1:T(8,128)S(1)} %get-tuple-element.204, bf16[8,1152,1,128]{3,1,2,0:T(8,128)(2,1)} %get-tuple-element.220, s32[]{:T(128)} %get-tuple-element.201, ...), kind=kOutput, calls=%fused_computation.8.clone.1 | convolution fusion | flops 342835200 | bytes 6792705 | tf_op jit(solution)/shard_map/while/body/eval_jaxpr/kgqs,skd->qkgd/dot_general | solution.py:29
  173.4 0.2 copy-done
  173.5 1.2 fusion.36
  174.8 0.3 broadcast_compare_fusion.3
  175.0 4.5 %fusion.34 = (f32[4,288]{1,0:T(4,128)S(1)}, f32[1,4,288,1152]{3,2,1,0:T(8,128)}) fusion(bf16[288,1,4,128]{3,0,2,1:T(8,128)(2,1)S(1)} %get-tuple-element.219, bf16[8,1152,1,128]{3,1,2,0:T(8,128)(2,1)} %get-tuple-element.218, s32[]{:T(128)} %get-tuple-element.201, pred[288,1152]{1,0:T(8,128)(4,1)S(1)} %broadcast_compare_fusion.3), kind=kOutput, calls=%fused_computation.36.clone.1 | convolution fusion | flops 343718784 | bytes 6235136 | tf_op jit(solution)/shard_map/while/body/eval_jaxpr/qkgd,skd->kgqs/dot_general | solution.py:20
  179.6 4.0 %fusion.37 = f32[288,1,4,128]{3,0,2,1:T(8,128)S(1)} fusion(f32[1,4,288,1152]{3,2,1,0:T(8,128)} %get-tuple-element.188, f32[4,288]{1,0:T(4,128)S(1)} %bitcast.82, f32[288,1,4,128]{3,0,2,1:T(8,128)S(1)} %get-tuple-element.204, bf16[8,1152,1,128]{3,1,2,0:T(8,128)(2,1)} %get-tuple-element.220, s32[]{:T(128)} %get-tuple-element.201, ...), kind=kOutput, calls=%fused_computation.8.clone.1 | convolution fusion | flops 342835200 | bytes 6792705 | tf_op jit(solution)/shard_map/while/body/eval_jaxpr/kgqs,skd->qkgd/dot_general | solution.py:29
  183.7 1.2 fusion.36
  185.0 0.3 broadcast_compare_fusion.3
  185.2 4.5 %fusion.34 = (f32[4,288]{1,0:T(4,128)S(1)}, f32[1,4,288,1152]{3,2,1,0:T(8,128)}) fusion(bf16[288,1,4,128]{3,0,2,1:T(8,128)(2,1)S(1)} %get-tuple-element.219, bf16[8,1152,1,128]{3,1,2,0:T(8,128)(2,1)} %get-tuple-element.218, s32[]{:T(128)} %get-tuple-element.201, pred[288,1152]{1,0:T(8,128)(4,1)S(1)} %broadcast_compare_fusion.3), kind=kOutput, calls=%fused_computation.36.clone.1 | convolution fusion | flops 343718784 | bytes 6235136 | tf_op jit(solution)/shard_map/while/body/eval_jaxpr/qkgd,skd->kgqs/dot_general | solution.py:20
  189.8 4.0 %fusion.37 = f32[288,1,4,128]{3,0,2,1:T(8,128)S(1)} fusion(f32[1,4,288,1152]{3,2,1,0:T(8,128)} %get-tuple-element.188, f32[4,288]{1,0:T(4,128)S(1)} %bitcast.82, f32[288,1,4,128]{3,0,2,1:T(8,128)S(1)} %get-tuple-element.204, bf16[8,1152,1,128]{3,1,2,0:T(8,128)(2,1)} %get-tuple-element.220, s32[]{:T(128)} %get-tuple-element.201, ...), kind=kOutput, calls=%fused_computation.8.clone.1 | convolution fusion | flops 342835200 | bytes 6792705 | tf_op jit(solution)/shard_map/while/body/eval_jaxpr/kgqs,skd->qkgd/dot_general | solution.py:29
  193.9 1.2 fusion.36
  195.2 0.3 broadcast_compare_fusion.3
  195.4 4.6 %fusion.34 = (f32[4,288]{1,0:T(4,128)S(1)}, f32[1,4,288,1152]{3,2,1,0:T(8,128)}) fusion(bf16[288,1,4,128]{3,0,2,1:T(8,128)(2,1)S(1)} %get-tuple-element.219, bf16[8,1152,1,128]{3,1,2,0:T(8,128)(2,1)} %get-tuple-element.218, s32[]{:T(128)} %get-tuple-element.201, pred[288,1152]{1,0:T(8,128)(4,1)S(1)} %broadcast_compare_fusion.3), kind=kOutput, calls=%fused_computation.36.clone.1 | convolution fusion | flops 343718784 | bytes 6235136 | tf_op jit(solution)/shard_map/while/body/eval_jaxpr/qkgd,skd->kgqs/dot_general | solution.py:20
  200.0 4.0 %fusion.37 = f32[288,1,4,128]{3,0,2,1:T(8,128)S(1)} fusion(f32[1,4,288,1152]{3,2,1,0:T(8,128)} %get-tuple-element.188, f32[4,288]{1,0:T(4,128)S(1)} %bitcast.82, f32[288,1,4,128]{3,0,2,1:T(8,128)S(1)} %get-tuple-element.204, bf16[8,1152,1,128]{3,1,2,0:T(8,128)(2,1)} %get-tuple-element.220, s32[]{:T(128)} %get-tuple-element.201, ...), kind=kOutput, calls=%fused_computation.8.clone.1 | convolution fusion | flops 342835200 | bytes 6792705 | tf_op jit(solution)/shard_map/while/body/eval_jaxpr/kgqs,skd->qkgd/dot_general | solution.py:29
  203.9 0.2 copy-done
  204.1 1.2 fusion.36
  205.4 0.3 broadcast_compare_fusion.3
  205.6 4.5 %fusion.34 = (f32[4,288]{1,0:T(4,128)S(1)}, f32[1,4,288,1152]{3,2,1,0:T(8,128)}) fusion(bf16[288,1,4,128]{3,0,2,1:T(8,128)(2,1)S(1)} %get-tuple-element.219, bf16[8,1152,1,128]{3,1,2,0:T(8,128)(2,1)} %get-tuple-element.218, s32[]{:T(128)} %get-tuple-element.201, pred[288,1152]{1,0:T(8,128)(4,1)S(1)} %broadcast_compare_fusion.3), kind=kOutput, calls=%fused_computation.36.clone.1 | convolution fusion | flops 343718784 | bytes 6235136 | tf_op jit(solution)/shard_map/while/body/eval_jaxpr/qkgd,skd->kgqs/dot_general | solution.py:20
  210.2 4.0 %fusion.37 = f32[288,1,4,128]{3,0,2,1:T(8,128)S(1)} fusion(f32[1,4,288,1152]{3,2,1,0:T(8,128)} %get-tuple-element.188, f32[4,288]{1,0:T(4,128)S(1)} %bitcast.82, f32[288,1,4,128]{3,0,2,1:T(8,128)S(1)} %get-tuple-element.204, bf16[8,1152,1,128]{3,1,2,0:T(8,128)(2,1)} %get-tuple-element.220, s32[]{:T(128)} %get-tuple-element.201, ...), kind=kOutput, calls=%fused_computation.8.clone.1 | convolution fusion | flops 342835200 | bytes 6792705 | tf_op jit(solution)/shard_map/while/body/eval_jaxpr/kgqs,skd->qkgd/dot_general | solution.py:29
  214.3 1.2 fusion.36
  215.5 0.3 broadcast_compare_fusion.3
  215.8 4.5 %fusion.34 = (f32[4,288]{1,0:T(4,128)S(1)}, f32[1,4,288,1152]{3,2,1,0:T(8,128)}) fusion(bf16[288,1,4,128]{3,0,2,1:T(8,128)(2,1)S(1)} %get-tuple-element.219, bf16[8,1152,1,128]{3,1,2,0:T(8,128)(2,1)} %get-tuple-element.218, s32[]{:T(128)} %get-tuple-element.201, pred[288,1152]{1,0:T(8,128)(4,1)S(1)} %broadcast_compare_fusion.3), kind=kOutput, calls=%fused_computation.36.clone.1 | convolution fusion | flops 343718784 | bytes 6235136 | tf_op jit(solution)/shard_map/while/body/eval_jaxpr/qkgd,skd->kgqs/dot_general | solution.py:20
  220.4 4.0 %fusion.37 = f32[288,1,4,128]{3,0,2,1:T(8,128)S(1)} fusion(f32[1,4,288,1152]{3,2,1,0:T(8,128)} %get-tuple-element.188, f32[4,288]{1,0:T(4,128)S(1)} %bitcast.82, f32[288,1,4,128]{3,0,2,1:T(8,128)S(1)} %get-tuple-element.204, bf16[8,1152,1,128]{3,1,2,0:T(8,128)(2,1)} %get-tuple-element.220, s32[]{:T(128)} %get-tuple-element.201, ...), kind=kOutput, calls=%fused_computation.8.clone.1 | convolution fusion | flops 342835200 | bytes 6792705 | tf_op jit(solution)/shard_map/while/body/eval_jaxpr/kgqs,skd->qkgd/dot_general | solution.py:29
  224.5 1.2 fusion.36
  225.7 0.3 broadcast_compare_fusion.3
  226.0 4.6 %fusion.34 = (f32[4,288]{1,0:T(4,128)S(1)}, f32[1,4,288,1152]{3,2,1,0:T(8,128)}) fusion(bf16[288,1,4,128]{3,0,2,1:T(8,128)(2,1)S(1)} %get-tuple-element.219, bf16[8,1152,1,128]{3,1,2,0:T(8,128)(2,1)} %get-tuple-element.218, s32[]{:T(128)} %get-tuple-element.201, pred[288,1152]{1,0:T(8,128)(4,1)S(1)} %broadcast_compare_fusion.3), kind=kOutput, calls=%fused_computation.36.clone.1 | convolution fusion | flops 343718784 | bytes 6235136 | tf_op jit(solution)/shard_map/while/body/eval_jaxpr/qkgd,skd->kgqs/dot_general | solution.py:20
  230.6 4.0 %fusion.37 = f32[288,1,4,128]{3,0,2,1:T(8,128)S(1)} fusion(f32[1,4,288,1152]{3,2,1,0:T(8,128)} %get-tuple-element.188, f32[4,288]{1,0:T(4,128)S(1)} %bitcast.82, f32[288,1,4,128]{3,0,2,1:T(8,128)S(1)} %get-tuple-element.204, bf16[8,1152,1,128]{3,1,2,0:T(8,128)(2,1)} %get-tuple-element.220, s32[]{:T(128)} %get-tuple-element.201, ...), kind=kOutput, calls=%fused_computation.8.clone.1 | convolution fusion | flops 342835200 | bytes 6792705 | tf_op jit(solution)/shard_map/while/body/eval_jaxpr/kgqs,skd->qkgd/dot_general | solution.py:29
  234.7 1.2 fusion.36
  235.9 0.3 broadcast_compare_fusion.3
  236.2 4.5 %fusion.34 = (f32[4,288]{1,0:T(4,128)S(1)}, f32[1,4,288,1152]{3,2,1,0:T(8,128)}) fusion(bf16[288,1,4,128]{3,0,2,1:T(8,128)(2,1)S(1)} %get-tuple-element.219, bf16[8,1152,1,128]{3,1,2,0:T(8,128)(2,1)} %get-tuple-element.218, s32[]{:T(128)} %get-tuple-element.201, pred[288,1152]{1,0:T(8,128)(4,1)S(1)} %broadcast_compare_fusion.3), kind=kOutput, calls=%fused_computation.36.clone.1 | convolution fusion | flops 343718784 | bytes 6235136 | tf_op jit(solution)/shard_map/while/body/eval_jaxpr/qkgd,skd->kgqs/dot_general | solution.py:20
  240.8 4.0 %fusion.37 = f32[288,1,4,128]{3,0,2,1:T(8,128)S(1)} fusion(f32[1,4,288,1152]{3,2,1,0:T(8,128)} %get-tuple-element.188, f32[4,288]{1,0:T(4,128)S(1)} %bitcast.82, f32[288,1,4,128]{3,0,2,1:T(8,128)S(1)} %get-tuple-element.204, bf16[8,1152,1,128]{3,1,2,0:T(8,128)(2,1)} %get-tuple-element.220, s32[]{:T(128)} %get-tuple-element.201, ...), kind=kOutput, calls=%fused_computation.8.clone.1 | convolution fusion | flops 342835200 | bytes 6792705 | tf_op jit(solution)/shard_map/while/body/eval_jaxpr/kgqs,skd->qkgd/dot_general | solution.py:29
  244.9 1.2 fusion.36
  246.1 0.4 select_convert_fusion
  246.6 7.4 %fusion.20 = bf16[7168,288]{0,1:T(8,128)(2,1)} fusion(bf16[512,7168]{1,0:T(8,128)(2,1)} %param.15, bf16[36,8,4,128]{3,2,1,0:T(4,128)(2,1)S(1)} %bitcast.86), kind=kOutput, calls=%fused_computation.25 | convolution fusion | flops 2115993600 | bytes 11763712 | tf_op jit(solution)/shard_map/dot_general | solution.py:99
  254.1 7.4 %copy.12 = bf16[7168,288]{1,0:T(8,128)(2,1)} copy(bf16[7168,288]{0,1:T(8,128)(2,1)} %fusion.20) | data formatting | bytes 8257536
  261.5 43.1 %reduce-scatter.4.cloned.1.call-done = bf16[896,288]{1,0:T(8,128)(2,1)} async-done(((bf16[7168,288]{1,0:T(8,128)(2,1)}), bf16[896,288]{1,0:T(8,128)(2,1)}) %reduce-scatter.4.cloned.1.call-update) | async-done | bytes 516112
  304.6 1.4 copy.13
  306.0 1.1 fusion.21
  (67 shorter events, 1.9 us)
Async XLA Ops:
  6.5 110.9 %all-gather.3.cloned.1.call-start = ((), (), s32[]{:S(2)}) async-start(), calls=%async_computation.1 | async-start | bytes 2433024 | tf_op jit(solution)/shard_map/all_gather | solution.py:74
  7.3 157.3 %all-gather.5.cloned.1.call-start = ((), (), s32[]{:S(2)}) async-start(), calls=%async_computation.2 | async-start | bytes 2433024 | tf_op jit(solution)/shard_map/all_gather | solution.py:75
  8.0 296.5 %reduce-scatter.4.cloned.1.call-start = ((), (), s32[]{:S(2)}) async-start(), calls=%async_computation.3 | async-start | bytes 6193152
  169.4 4.2 %copy-start = (f32[1,4,288,1152]{3,2,1,0:T(8,128)S(1)}, f32[1,4,288,1152]{3,2,1,0:T(8,128)}, u32[]{:S(2)}) copy-start(f32[1,4,288,1152]{3,2,1,0:T(8,128)} %get-tuple-element.188) | copy-start | bytes 15925252 | tf_op jit(solution)/shard_map/while
  179.6 4.2 %copy-start = (f32[1,4,288,1152]{3,2,1,0:T(8,128)S(1)}, f32[1,4,288,1152]{3,2,1,0:T(8,128)}, u32[]{:S(2)}) copy-start(f32[1,4,288,1152]{3,2,1,0:T(8,128)} %get-tuple-element.188) | copy-start | bytes 15925252 | tf_op jit(solution)/shard_map/while
  189.8 4.2 %copy-start = (f32[1,4,288,1152]{3,2,1,0:T(8,128)S(1)}, f32[1,4,288,1152]{3,2,1,0:T(8,128)}, u32[]{:S(2)}) copy-start(f32[1,4,288,1152]{3,2,1,0:T(8,128)} %get-tuple-element.188) | copy-start | bytes 15925252 | tf_op jit(solution)/shard_map/while
  200.0 4.2 %copy-start = (f32[1,4,288,1152]{3,2,1,0:T(8,128)S(1)}, f32[1,4,288,1152]{3,2,1,0:T(8,128)}, u32[]{:S(2)}) copy-start(f32[1,4,288,1152]{3,2,1,0:T(8,128)} %get-tuple-element.188) | copy-start | bytes 15925252 | tf_op jit(solution)/shard_map/while
  210.2 4.2 %copy-start = (f32[1,4,288,1152]{3,2,1,0:T(8,128)S(1)}, f32[1,4,288,1152]{3,2,1,0:T(8,128)}, u32[]{:S(2)}) copy-start(f32[1,4,288,1152]{3,2,1,0:T(8,128)} %get-tuple-element.188) | copy-start | bytes 15925252 | tf_op jit(solution)/shard_map/while
  220.4 4.2 %copy-start = (f32[1,4,288,1152]{3,2,1,0:T(8,128)S(1)}, f32[1,4,288,1152]{3,2,1,0:T(8,128)}, u32[]{:S(2)}) copy-start(f32[1,4,288,1152]{3,2,1,0:T(8,128)} %get-tuple-element.188) | copy-start | bytes 15925252 | tf_op jit(solution)/shard_map/while
  230.5 4.2 %copy-start = (f32[1,4,288,1152]{3,2,1,0:T(8,128)S(1)}, f32[1,4,288,1152]{3,2,1,0:T(8,128)}, u32[]{:S(2)}) copy-start(f32[1,4,288,1152]{3,2,1,0:T(8,128)} %get-tuple-element.188) | copy-start | bytes 15925252 | tf_op jit(solution)/shard_map/while
  240.7 4.2 %copy-start = (f32[1,4,288,1152]{3,2,1,0:T(8,128)S(1)}, f32[1,4,288,1152]{3,2,1,0:T(8,128)}, u32[]{:S(2)}) copy-start(f32[1,4,288,1152]{3,2,1,0:T(8,128)} %get-tuple-element.188) | copy-start | bytes 15925252 | tf_op jit(solution)/shard_map/while
  254.1 7.4 %copy-start.2 = (s32[288]{0:T(512)S(1)}, s32[288]{0:T(512)}, u32[]{:S(2)}) copy-start(s32[288]{0:T(512)} %param.10) | copy-start | bytes 3460
  261.4 44.5 %copy-start.1 = (bf16[288,896]{1,0:T(8,128)(2,1)S(1)}, bf16[288,896]{1,0:T(8,128)(2,1)}, u32[]{:S(2)}) copy-start(bf16[288,896]{1,0:T(8,128)(2,1)} %param.9) | copy-start | bytes 1548292
  261.4 44.5 %copy-start.3 = (f32[288]{0:T(512)S(1)}, f32[288]{0:T(512)}, u32[]{:S(2)}) copy-start(f32[288]{0:T(512)} %param.11) | copy-start | bytes 3460
Sparse Core Ops, SparseCore 0:
  9.9 76.0 all-gather.2
  88.7 75.8 all-gather.4
  261.6 42.9 reduce-scatter.3
where the time goes:
time: 317 us; the launch traced here: 314 us
  blocking collectives  105 us (33%)
  waiting for transfers between devices  91.6 us (29%)
  matrix products  75.5 us (24%)
  between operations  13.9 us (4%)
  other arithmetic  13.7 us (4%)
  local copies, waits for them, and re-layouts  13 us (4%)
    unnamed x1, blocking collectives  105 us
    all_gather x1, waiting for transfers between devices, local(): value_piece = lax.all_gather(values, 'context', axis=0, tiled=True)  47.1 us
    unnamed x4, waiting for transfers between devices  44.5 us
    dot_general x8, matrix products, online_step(): jnp.einsum('qkgd,skd->kgqs', query_block, key_block, preferred_element_ty...  36.4 us
    dot_general x8, matrix products, online_step(): jnp.einsum('kgqs,skd->qkgd', weights.astype(jnp.bfloat16), value_block, p...  31.6 us
    unnamed x11, local copies, waits for them, and re-layouts  10.1 us
    reduce_sum x8, other arithmetic, online_step(): row_total = factor * row_total + jnp.sum(weights, axis=-1)  9.23 us
    dot_general x1, matrix products, local(): lax.dot_general(out_weight, attended, (((0,), (1,)), ((), ())), preferred...  7.41 us
  transfers between devices with their start and end apart: 3, of which 2 were waited for; matrix products, arithmetic and copies ran while one was open for 1% of the time, Pallas kernels for 0%

commit v1 on v0

v1 whole, which is shorter than its diff:
```python
import jax
import jax.numpy as jnp
from jax import lax
from jax.experimental import pallas as pl
from jax.experimental.pallas import tpu as pltpu
from jax.sharding import PartitionSpec as P

MESH = pl.DeviceIdType.MESH

TOK_DEV = 1536
CAP = 288
HD = 128
NY, NZ, NX = 4, 8, 4
WIDTH = 896
GROUP = 4
KAPPA = 128**-0.5 * 1.4426950408889634
NEG = -1e30
FILL = 64.0
TILE = 144

ROWS = {"A": 160, "B": 128}
FIRST = {"A": 0, "B": 160}
TURNS = {"A": (4, 3), "B0": (3, 4), "Bm": (4, 3), "Bp": (3, 4), "B2": (4, 3)}
ROW_OF = {"A": 0, "B0": 0, "Bm": 3, "Bp": 1, "B2": 2}
OFFSETS = (0, -1, -2, -3, 4, 1, 2, 3)
UPWARDS = (0, -1, -2, -3)

ORDER = (
    ("c", "diag", 0), ("c", "diag", 1),
    ("w", "YB", "P"), ("w", "YB", "M"), ("w", "ZR", "A", 1), ("w", "ZL", "A", 1), ("w", "YP", 0), ("w", "YM", 0),
    ("w", "ZR", "B0", 1), ("w", "ZL", "B0", 1), ("w", "YB", "2"), ("w", "ZL", "Bp", 1), ("w", "ZR", "A", 2),
    ("w", "YM", -1), ("w", "YP", -1), ("w", "ZR", "Bp", 1), ("w", "ZL", "A", 2), ("w", "YM", 1), ("w", "ZR", "B0", 2),
    ("w", "ZL", "B0", 2), ("w", "YP", 1), ("w", "YM", -2), ("w", "ZL", "Bp", 2), ("w", "ZR", "A", 3), ("w", "YP2", 0),
    ("w", "YM", 2), ("w", "ZR", "Bp", 2), ("w", "ZL", "A", 3), ("w", "YP", -2), ("w", "YM2", 1), ("w", "ZR", "B0", 3),
    ("w", "ZL", "B0", 3), ("w", "YP2", -1), ("w", "ZL", "Bp", 3), ("w", "YM", -3), ("w", "ZR", "A", 4),
    ("c", "A", 0, 0), ("w", "YP", 2), ("w", "ZL", "B0", 4), ("c", "A", 0, 1), ("w", "YM2", 2), ("w", "ZR", "Bp", 3),
    ("c", "B", 0, 0), ("w", "ZL", "Bp", 4), ("w", "YP", -3), ("w", "ZR", "Bm", 1), ("w", "YM", 3), ("c", "B", 0, 1),
    ("w", "ZL", "Bm", 1), ("c", "B", 1, 0), ("w", "ZR", "B2", 1), ("w", "YP", 3), ("w", "YM", 4), ("c", "B", 1, 1),
    ("w", "ZL", "B2", 1), ("w", "ZR", "Bm", 2), ("c", "A", 1, 0), ("w", "YP2", -2), ("w", "YM2", 3), ("w", "ZL", "Bm", 2),
    ("c", "A", 1, 1), ("w", "ZR", "B2", 2), ("w", "YP", 4), ("c", "A", 3, 0), ("w", "YM2", 4), ("w", "ZL", "B2", 2),
    ("w", "ZR", "Bm", 3), ("c", "A", 3, 1), ("w", "YP2", -3), ("w", "ZL", "Bm", 3), ("c", "A", 2, 0), ("w", "ZR", "B2", 3),
    ("c", "A", 2, 1), ("w", "ZL", "B2", 3), ("w", "ZR", "Bm", 4), ("c", "B", 3, 0), ("c", "B", 3, 1), ("w", "ZR", "B2", 4),
    ("c", "B", 2, 0), ("c", "B", 2, 1),
)
OPENS = {("ZR", "A", 4): ("Bm",), ("YB", "M"): ("Bp",), ("ZL", "B0", 4): ("B2",)}

Z_IDS = [(side, s, i + 1) for s, (r, l) in TURNS.items() for side, n in (("ZR", r), ("ZL", l)) for i in range(n)]
Y_IDS = [(kind, o) for kind in ("YP", "YM") for o in OFFSETS]
Y_IDS += [("YP2", o) for o in UPWARDS] + [("YM2", o) for o in OFFSETS if o not in UPWARDS]
Y_IDS += [("YB", "P"), ("YB", "M"), ("YB", "2")]
G_IDS = Z_IDS + Y_IDS
N_GATHER = len(G_IDS)
NUMBER = {name: i for i, name in enumerate(G_IDS)}


def kernel(
    q_ref, k_ref, v_ref, picks_ref, router_ref, stream_ref, w_hbm, out_ref,
    part_a, part_b, va, row_max, acc, w, att, sib_out, sib_in, hop_out, hop_in, end_out, end_in, total,
    send_sem, recv_sem, sib_send, sib_recv, x_send, x_recv, w_sem,
):
    ctx, ten = lax.axis_index("context"), lax.axis_index("tensor")
    y, z = ctx // NZ, lax.rem(ctx, NZ)
    x, core = ten // 2, lax.rem(ten, 2)

    def wrap(i, n):
        return lax.rem(i + 2 * n, n)

    def at_ctx(yy, zz):
        return (wrap(yy, NY) * NZ + wrap(zz, NZ), ten)

    def at_ten(xx, cc):
        return (ctx, wrap(xx, NX) * 2 + cc)

    up, down, right, left = at_ctx(y + 1, z), at_ctx(y - 1, z), at_ctx(y, z + 1), at_ctx(y, z - 1)
    sibling, x_up, x_down = at_ten(x, 1 - core), at_ten(x + 1, core), at_ten(x - 1, core)

    w_copy = pltpu.make_async_copy(w_hbm, w, w_sem)
    w_copy.start()

    barrier = pltpu.get_barrier_semaphore()
    peers = (up, down, right, left, sibling, x_up, x_down)
    for peer in peers:
        pl.semaphore_signal(barrier, inc=1, device_id=peer, device_id_type=MESH)

    count = jnp.sum(jnp.where(picks_ref[...] < TOK_DEV, 1.0, 0.0), axis=1, keepdims=True)
    row_id = lax.broadcasted_iota(jnp.int32, (CAP, HD), 0)
    valid = row_id.astype(jnp.float32) < count
    k_all, v_all = k_ref[...], v_ref[...]
    k_out = jnp.where(valid, k_all.astype(jnp.float32), k_all[:1].astype(jnp.float32)).astype(jnp.bfloat16)
    v_out = jnp.where(valid, v_all.astype(jnp.float32), FILL).astype(jnp.bfloat16)

    def slot(part, yy, zz):
        rows = ROWS[part]
        start = pl.multiple_of((wrap(yy, NY) * NZ + wrap(zz, NZ)) * rows, 16)
        return (part_a if part == "A" else part_b).at[pl.ds(start, rows), :]

    for part in ("A", "B"):
        rows = slice(FIRST[part], FIRST[part] + ROWS[part])
        own = slot(part, y, z)
        own[:, :HD] = k_out[rows]
        own[:, HD:] = v_out[rows]

    def ends(name):
        kind = name[0]
        if kind in ("ZR", "ZL"):
            _, stream, step = name
            part, yy = stream[0], y + ROW_OF[stream]
            if kind == "ZR":
                return slot(part, yy, z - step + 1), slot(part, yy, z - step), right
            return slot(part, yy, z + step - 1), slot(part, yy, z + step), left
        if kind == "YB":
            if name[1] == "P":
                return slot("B", y, z), slot("B", y - 1, z), up
            if name[1] == "M":
                return slot("B", y, z), slot("B", y + 1, z), down
            return slot("B", y - 1, z), slot("B", y - 2, z), up
        zz = z + name[1]
        if kind == "YP":
            return slot("A", y, zz), slot("A", y - 1, zz), up
        if kind == "YM":
            return slot("A", y, zz), slot("A", y + 1, zz), down
        if kind == "YP2":
            return slot("A", y - 1, zz), slot("A", y - 2, zz), up
        return slot("A", y + 1, zz), slot("A", y + 2, zz), down

    def outgoing(name):
        i = NUMBER[name]
        src, _, target = ends(name)
        return pltpu.make_async_remote_copy(
            src, src, send_sem.at[i], recv_sem.at[i], device_id=target, device_id_type=MESH
        )

    def incoming(name):
        i = NUMBER[name]
        _, dst, target = ends(name)
        return pltpu.make_async_remote_copy(
            dst, dst, send_sem.at[i], recv_sem.at[i], device_id=target, device_id_type=MESH
        )

    def start(name):
        outgoing(name).start()

    def open_ring(stream):
        start(("ZR", stream, 1))
        start(("ZL", stream, 1))

    def arrive(name):
        incoming(name).wait_recv()
        kind = name[0]
        if kind in ("ZR", "ZL"):
            _, stream, step = name
            if step < TURNS[stream][0 if kind == "ZR" else 1]:
                start((kind, stream, step + 1))
            if stream == "A":
                offset = step if kind == "ZL" else (-step if step < 4 else 4)
                start(("YP", offset))
                start(("YM", offset))
        elif kind == "YP" and name[1] in UPWARDS:
            start(("YP2", name[1]))
        elif kind == "YM" and name[1] not in UPWARDS:
            start(("YM2", name[1]))
        elif name == ("YB", "P"):
            start(("YB", "2"))
        for stream in OPENS.get(name, ()):
            open_ring(stream)

    def q_tile(t):
        g, half = t // 2, t % 2
        return q_ref[half * TILE : (half + 1) * TILE, g * HD : (g + 1) * HD]

    def qk(t, keys):
        return lax.dot_general(q_tile(t), keys, (((1,), (1,)), ((), ())), preferred_element_type=jnp.float32)

    def diagonal(half):
        if half == 0:
            va[:CAP, :HD] = v_ref[...]
            va[:CAP, HD:] = jnp.ones((CAP, HD), jnp.bfloat16)
        for t in range(half * 4, half * 4 + 4):
            rows = pl.ds(t * TILE, TILE)
            scores = qk(t, k_ref[...])
            i = lax.broadcasted_iota(jnp.int32, scores.shape, 0) + (t % 2) * TILE
            j = lax.broadcasted_iota(jnp.int32, scores.shape, 1)
            scores = jnp.where(j <= i, scores, NEG)
            top = jnp.max(scores, axis=1, keepdims=True)
            weights = jnp.exp2((scores - top) * KAPPA).astype(jnp.bfloat16)
            acc[rows, :] = jnp.dot(weights, va[:CAP, :], preferred_element_type=jnp.float32)
            row_max[rows, :] = jnp.broadcast_to(top, (TILE, HD))

    def unit(part, rho, half):
        n = NZ * ROWS[part]
        yy = wrap(y + rho, NY)
        first = pl.multiple_of(yy * n, n)
        ref = part_a if part == "A" else part_b

        @pl.when(z > 0 if rho == 0 else yy < y)
        def _():
            if half == 0:
                block = ref[pl.ds(first, n), HD:]
                real = block < FILL / 2
                va[:n, :HD] = jnp.where(real, block, 0).astype(jnp.bfloat16)
                va[:n, HD:] = jnp.where(real, 1, 0).astype(jnp.bfloat16)
            for t in range(half * 4, half * 4 + 4):
                rows = pl.ds(t * TILE, TILE)
                scores = qk(t, ref[pl.ds(first, n), :HD])
                if rho == 0:
                    j = lax.broadcasted_iota(jnp.int32, scores.shape, 1)
                    scores = jnp.where(j < z * ROWS[part], scores, NEG)
                old = row_max[rows, :]
                new = jnp.maximum(old, jnp.max(scores, axis=1, keepdims=True))
                weights = jnp.exp2((scores - new[:, :1]) * KAPPA).astype(jnp.bfloat16)
                factor = jnp.exp2((old - new) * KAPPA)
                more = jnp.dot(weights, va[:n, :], preferred_element_type=jnp.float32)
                acc[rows, :HD] = acc[rows, :HD] * factor + more[:, :HD]
                acc[rows, HD:] = acc[rows, HD:] * factor + more[:, HD:]
                row_max[rows, :] = new

    pl.semaphore_wait(barrier, len(peers))
    start(("YB", "P"))
    start(("YB", "M"))
    open_ring("A")
    start(("YP", 0))
    start(("YM", 0))
    open_ring("B0")

    for what, *rest in ORDER:
        if what == "w":
            arrive(tuple(rest))
        elif rest[0] == "diag":
            diagonal(rest[1])
        else:
            unit(*rest)

    for t in range(8):
        g, half = t // 2, t % 2
        rows = pl.ds(t * TILE, TILE)
        att[half * TILE : (half + 1) * TILE, g * HD : (g + 1) * HD] = (acc[rows, :HD] / acc[rows, HD:]).astype(jnp.bfloat16)

    w_copy.wait()

    def partial(d, cc):
        cols = pl.ds(pl.multiple_of((wrap(x + d, NX) * 2 + cc) * WIDTH, 128), WIDTH)
        return jnp.dot(att[...], w[:, cols], preferred_element_type=jnp.float32)

    def to_sibling(d):
        return pltpu.make_async_remote_copy(
            sib_out.at[d], sib_in.at[d], sib_send.at[d], sib_recv.at[d], device_id=sibling, device_id_type=MESH
        )

    lo, hi = pl.ds(0, TILE), pl.ds(TILE, TILE)

    def x_copy(i, src, dst, target):
        return pltpu.make_async_remote_copy(
            src, dst, x_send.at[i], x_recv.at[i], device_id=target, device_id_type=MESH
        )

    hop_up = x_copy(0, hop_out.at[lo], hop_in.at[lo], x_up)
    hop_down = x_copy(1, hop_out.at[hi], hop_in.at[hi], x_down)
    up_hi = x_copy(2, end_out.at[0, hi], end_in.at[0, hi], x_up)
    up_lo = x_copy(3, end_out.at[0, lo], end_in.at[0, lo], x_up)
    down_lo = x_copy(4, end_out.at[1, lo], end_in.at[1, lo], x_down)
    down_hi = x_copy(5, end_out.at[1, hi], end_in.at[1, hi], x_down)

    def send_sibling(d):
        sib_out[d] = partial(d, 1 - core).astype(jnp.bfloat16)
        to_sibling(d).start()

    def chip_sum(d):
        own = partial(d, core)
        to_sibling(d).wait_recv()
        return own + sib_in[d].astype(jnp.float32)

    send_sibling(2)
    send_sibling(1)
    hop_out[...] = chip_sum(2).astype(jnp.bfloat16)
    hop_up.start()
    hop_down.start()
    send_sibling(3)
    total[...] = chip_sum(1)
    end_out[0, hi] = total[hi, :].astype(jnp.bfloat16)
    up_hi.start()
    hop_up.wait_recv()
    end_out[0, lo] = (total[lo, :] + hop_in[lo, :].astype(jnp.float32)).astype(jnp.bfloat16)
    up_lo.start()
    total[...] = chip_sum(3)
    end_out[1, lo] = total[lo, :].astype(jnp.bfloat16)
    down_lo.start()
    hop_down.wait_recv()
    end_out[1, hi] = (total[hi, :] + hop_in[hi, :].astype(jnp.float32)).astype(jnp.bfloat16)
    down_hi.start()
    send_sibling(0)
    total[...] = chip_sum(0)

    router = router_ref[...]
    eye = lax.broadcasted_iota(jnp.int32, (CAP, CAP), 0) == lax.broadcasted_iota(jnp.int32, (CAP, CAP), 1)
    gain = jnp.sum(jnp.where(eye, router, 0.0), axis=1, keepdims=True)
    wide_valid = lax.broadcasted_iota(jnp.int32, (CAP, WIDTH), 0).astype(jnp.float32) < count

    def finish(rows, first, second):
        first.wait_recv()
        second.wait_recv()
        here = slice(0, TILE) if rows is lo else slice(TILE, CAP)
        projected = total[rows, :] + end_in[0, rows].astype(jnp.float32) + end_in[1, rows].astype(jnp.float32)
        residual = stream_ref[rows, :].astype(jnp.float32)
        updated = jnp.where(wide_valid[here], residual + gain[here] * projected, residual)
        out_ref[rows, :] = updated.astype(jnp.bfloat16)

    finish(lo, down_lo, up_lo)
    finish(hi, up_hi, down_hi)

    for name in G_IDS:
        outgoing(name).wait_send()
    for d in range(NX):
        to_sibling(d).wait_send()
    for copy in (hop_up, hop_down, up_hi, up_lo, down_lo, down_hi):
        copy.wait_send()


def local(stream_rows, picks, router, queries, keys, values, out_weight):
    vmem = pl.BlockSpec(memory_space=pltpu.VMEM)
    bf16, f32 = jnp.bfloat16, jnp.float32
    dma = pltpu.SemaphoreType.DMA
    return pl.pallas_call(
        kernel,
        out_shape=jax.ShapeDtypeStruct(stream_rows.shape, bf16),
        in_specs=[vmem] * 6 + [pl.BlockSpec(memory_space=pl.ANY)],
        out_specs=vmem,
        scratch_shapes=[
            pltpu.VMEM((NY * NZ * ROWS["A"], 2 * HD), bf16),
            pltpu.VMEM((NY * NZ * ROWS["B"], 2 * HD), bf16),
            pltpu.VMEM((NZ * ROWS["A"], 2 * HD), bf16),
            pltpu.VMEM((GROUP * CAP, HD), f32),
            pltpu.VMEM((GROUP * CAP, 2 * HD), f32),
            pltpu.VMEM(out_weight.shape, bf16),
            pltpu.VMEM((CAP, GROUP * HD), bf16),
            pltpu.VMEM((NX, CAP, WIDTH), bf16),
            pltpu.VMEM((NX, CAP, WIDTH), bf16),
            pltpu.VMEM((CAP, WIDTH), bf16),
            pltpu.VMEM((CAP, WIDTH), bf16),
            pltpu.VMEM((2, CAP, WIDTH), bf16),
            pltpu.VMEM((2, CAP, WIDTH), bf16),
            pltpu.VMEM((CAP, WIDTH), f32),
            dma((N_GATHER,)),
            dma((N_GATHER,)),
            dma((NX,)),
            dma((NX,)),
            dma((6,)),
            dma((6,)),
            dma,
        ],
        compiler_params=pltpu.CompilerParams(
            collective_id=0, has_side_effects=True, vmem_limit_bytes=56 * 2**20
        ),
        cost_estimate=pl.CostEstimate(flops=8 * 10**9, bytes_accessed=10**7, transcendentals=10**7),
    )(queries, keys, values, picks.reshape(1, CAP), router.reshape(1, CAP), stream_rows, out_weight)


def solution(mesh):
    placed = (
        P("context", "tensor"),
        P("context"),
        P("context"),
        P("context", "tensor"),
        P("context", "tensor"),
        P("context", "tensor"),
        P("tensor", None),
    )
    return jax.shard_map(
        local, mesh=mesh, in_specs=placed, out_specs=P("context", "tensor"), check_vma=False
    )
```

time: 317 us -> 81.2 us (0.26)
  blocking collectives: 105 us -> 0 us
  waiting for transfers between devices: 91.6 us -> 0 us
  Pallas kernels: 0 us -> 76.4 us
  matrix products: 75.5 us -> 0 us
  between operations: 13.9 us -> 0.01 us
  other arithmetic: 13.7 us -> 0 us
  local copies, waits for them, and re-layouts: 13 us -> 4.39 us
    unnamed x1 -> x0, blocking collectives: 105 us -> none
    pallas_call x0 -> x1, Pallas kernels: none -> 76.4 us  [local(): pl.pallas_call(kernel, out_shape=jax.ShapeDtypeStruct(stream_rows.shape,...]
    dot_general x17 -> x0, matrix products: 75.5 us -> none  [the longest x8 36.4 us: online_step(): jnp.einsum('qkgd,skd->kgqs', query_block, key_block, preferred_element_ty...]
    all_gather x2 -> x0, waiting for transfers between devices: 47.1 us -> none  [the longest x1 47.1 us: local(): value_piece = lax.all_gather(values, 'context', axis=0, tiled=True)]
    unnamed x4 -> x0, waiting for transfers between devices: 44.5 us -> none
    reduce_sum x8 -> x0, other arithmetic: 9.23 us -> none  [online_step(): row_total = factor * row_total + jnp.sum(weights, axis=-1)]
    unnamed x11 -> x1, local copies, waits for them, and re-layouts: 10.1 us -> 1.87 us
  transfers between devices with their start and end apart: 3 -> 0, of which waited for: 2 -> 0; matrix products, arithmetic and copies ran while one was open for 1% -> 0% of each run, Pallas kernels for 0% -> 0%
where the time goes in v1:
time: 81.2 us; the launch traced here: 80.8 us
  Pallas kernels  76.4 us (94%)
  local copies, waits for them, and re-layouts  4.39 us (5%)
    pallas_call x1, Pallas kernels, local(): pl.pallas_call(kernel, out_shape=jax.ShapeDtypeStruct(stream_rows.shape,...  76.4 us
    unnamed x1, local copies, waits for them, and re-layouts  1.87 us

profile of v1, /device:TPU:25, one launch (start us, length us, event | category | flops | bytes accessed | tf_op | source)
XLA Modules:
  0.0 80.8 jit_solution(16766828009191213002)
XLA Ops:
  0.0 1.2 %reshape.6.picks_ref = s32[1,288]{1,0:T(1,128)} reshape(s32[288]{0:T(512)} %param.8) | data formatting | bytes 2304 | tf_op jit(solution)/shard_map/reshape | solution.py:354
  1.2 1.3 %reshape.7.router_ref = f32[1,288]{1,0:T(1,128)} reshape(f32[288]{0:T(512)} %param.9) | data formatting | bytes 2304 | tf_op jit(solution)/shard_map/reshape | solution.py:354
  2.5 76.4 %shard_map.73 = bf16[288,896]{1,0:T(8,128)(2,1)} custom-call(bf16[288,512]{1,0:T(8,128)(2,1)} %q_ref.1, bf16[288,128]{1,0:T(8,128)(2,1)} %k_ref.1, bf16[288,128]{1,0:T(8,128)(2,1)} %v_ref.1, s32[1,288]{1,0:T(1,128)} %reshape.6.picks_ref, f32[1,288]{1,0:T(1,128)} %reshape.7.router_ref, bf16[288,896]{1,0:T(8,128)(2,1)} %stream_ref.1, bf16[512,7168]{1,0:T(8,128)(2,1)} %w_hbm.1), custom_call_target="tpu_custom_call" | custom-call | flops 8000000000 | bytes 10000000 | tf_op jit(solution)/shard_map/pallas_call | solution.py:322
  78.9 1.9 %copy.9 = bf16[288,896]{1,0:T(8,128)(2,1)} copy(bf16[288,896]{1,0:T(8,128)(2,1)} %shard_map.73) | data formatting | bytes 1032192

commit v2 on v1

v2 whole, which is shorter than its diff:
```python
import jax
import jax.numpy as jnp
from jax import lax
from jax.experimental import pallas as pl
from jax.experimental.pallas import tpu as pltpu
from jax.sharding import PartitionSpec as P

MESH = pl.DeviceIdType.MESH

TOK_DEV = 1536
CAP = 288
HD = 128
NY, NZ, NX = 4, 8, 4
WIDTH = 896
GROUP = 4
KAPPA = 128**-0.5 * 1.4426950408889634
NEG = -1e30
FILL = 64.0
TILE = 144

ROWS = {"A": 176, "B": 112}
FIRST = {"A": 0, "B": 176}
TURNS = {"A": (4, 3), "B0": (4, 3), "Bm": (3, 4), "Bp": (3, 4), "B2": (3, 4)}
ROW_OF = {"A": 0, "B0": 0, "Bm": 3, "Bp": 1, "B2": 2}
OFFSETS = (0, -1, -2, -3, 4, 1, 2, 3)
UPWARDS = (0, -1, -2, -3)
FIRST_SENDS = ("YB", "A", "YA", "B0")
UNITS = (
    (("YB", "P"), ("YB", "M"), ("ZR", "A", 1), ("ZL", "A", 1),),
    (("YP", 0), ("YM", 0), ("ZR", "B0", 1), ("ZL", "B0", 1),),
    (("YB", "2"), ("ZR", "A", 2), ("YM", -1), ("ZL", "A", 2),),
    (("YP", -1), ("ZR", "B0", 2), ("ZL", "B0", 2), ("YM", 1),),
    (("YP", 1), ("ZR", "Bp", 1), ("ZL", "Bp", 1), ("ZL", "B2", 1),),
    (("YM", -2), ("YP2", 0), ("ZR", "A", 3),),
    (("ZR", "B2", 1), ("ZL", "A", 3), ("YM", 2), ("YP", -2), ("ZR", "Bm", 1),),
    (("ZL", "Bm", 1), ("YM2", 1), ("ZR", "B0", 3), ("ZL", "B0", 3),),
    (("YP", 2), ("ZR", "Bp", 2), ("ZL", "Bp", 2), ("YM", -3), ("YP2", -1),),
    (("ZL", "B2", 2), ("ZR", "A", 4), ("ZL", "Bm", 2), ("YM", 3), ("YP", -3),),
    (("ZR", "B2", 2), ("ZL", "Bp", 3), ("ZR", "Bm", 2), ("YM2", 2),),
    (("YP", 3), ("ZL", "B2", 3), ("ZR", "B0", 4), ("YM", 4), ("ZL", "Bm", 3), ("YP2", -2), ("ZR", "Bp", 3),),
    (("ZL", "Bp", 4), ("ZR", "B2", 3), ("YM2", 3), ("YP", 4), ("ZL", "B2", 4),),
    (("ZR", "Bm", 3), ("ZL", "Bm", 4), ("YP2", -3), ("YM2", 4),),
)
ORDER = (
    ("c", "diag", 0), ("c", "diag", 1), ("w", "YB", "P"), ("w", "YB", "M"), ("w", "ZR", "A", 1), ("w", "ZL", "A", 1),
    ("c", 0, 0), ("c", 0, 1), ("w", "YP", 0), ("w", "YM", 0), ("w", "ZR", "B0", 1), ("w", "ZL", "B0", 1),
    ("c", 1, 0), ("c", 1, 1), ("w", "YB", "2"), ("w", "ZR", "A", 2), ("w", "YM", -1), ("w", "ZL", "A", 2),
    ("c", 2, 0), ("w", "YP", -1), ("c", 2, 1), ("w", "ZR", "B0", 2), ("w", "ZL", "B0", 2), ("w", "YM", 1),
    ("c", 3, 0), ("w", "YP", 1), ("w", "ZR", "Bp", 1), ("w", "ZL", "Bp", 1), ("c", 3, 1), ("w", "ZL", "B2", 1),
    ("c", 4, 0), ("w", "YM", -2), ("w", "YP2", 0), ("w", "ZR", "A", 3), ("c", 4, 1), ("c", 5, 0),
    ("w", "ZR", "B2", 1), ("w", "ZL", "A", 3), ("w", "YM", 2), ("c", 5, 1), ("w", "YP", -2), ("w", "ZR", "Bm", 1),
    ("w", "ZL", "Bm", 1), ("c", 6, 0), ("w", "YM2", 1), ("w", "ZR", "B0", 3), ("w", "ZL", "B0", 3), ("w", "YP", 2),
    ("c", 6, 1), ("c", 7, 0), ("w", "ZR", "Bp", 2), ("w", "ZL", "Bp", 2), ("c", 7, 1), ("w", "YM", -3),
    ("w", "YP2", -1), ("w", "ZL", "B2", 2), ("c", 8, 0), ("w", "ZR", "A", 4), ("c", 8, 1), ("w", "ZL", "Bm", 2),
    ("w", "YM", 3), ("w", "YP", -3), ("w", "ZR", "B2", 2), ("c", 9, 0), ("w", "ZL", "Bp", 3), ("c", 9, 1),
    ("w", "ZR", "Bm", 2), ("w", "YM2", 2), ("w", "YP", 3), ("w", "ZL", "B2", 3), ("c", 10, 0), ("w", "ZR", "B0", 4),
    ("c", 10, 1), ("w", "YM", 4), ("w", "ZL", "Bm", 3), ("w", "YP2", -2), ("w", "ZR", "Bp", 3), ("c", 11, 0),
    ("w", "ZL", "Bp", 4), ("w", "ZR", "B2", 3), ("c", 11, 1), ("w", "YM2", 3), ("w", "YP", 4), ("w", "ZL", "B2", 4),
    ("w", "ZR", "Bm", 3), ("c", 12, 0), ("w", "ZL", "Bm", 4), ("c", 12, 1), ("w", "YP2", -3), ("w", "YM2", 4),
    ("c", 13, 0), ("c", 13, 1),
)
OPENS = {
    ("ZL", "B0", 1): ("Bp",),
    ("ZR", "A", 2): ("B2",),
    ("ZL", "A", 2): ("Bm",),
}

Z_IDS = [(side, s, i + 1) for s, (r, l) in TURNS.items() for side, n in (("ZR", r), ("ZL", l)) for i in range(n)]
Y_IDS = [(kind, o) for kind in ("YP", "YM") for o in OFFSETS]
Y_IDS += [("YP2", o) for o in UPWARDS] + [("YM2", o) for o in OFFSETS if o not in UPWARDS]
Y_IDS += [("YB", "P"), ("YB", "M"), ("YB", "2")]
G_IDS = Z_IDS + Y_IDS
N_GATHER = len(G_IDS)
NUMBER = {name: i for i, name in enumerate(G_IDS)}


def part_of(name):
    return "A" if name[1] == "A" or (name[0][0] == "Y" and name[0] != "YB") else "B"


PLACE, UNIT_ROWS = {}, []
for unit_pieces in UNITS:
    begin = sum(UNIT_ROWS)
    end = begin
    for piece in unit_pieces:
        PLACE[piece] = end
        end += ROWS[part_of(piece)]
    UNIT_ROWS.append(end - begin)

BLOCKS = (((0, 80), (80, 64)), ((144, 64), (208, 80)))


def kernel(
    q_ref, k_ref, v_ref, picks_ref, router_ref, stream_ref, w_hbm, out_ref,
    own, held, va, row_max, acc, w, att, sib_out, sib_in, hop_out, hop_in, end_out, end_in, total,
    send_sem, recv_sem, sib_send, sib_recv, x_send, x_recv, w_sem,
):
    ctx, ten = lax.axis_index("context"), lax.axis_index("tensor")
    y, z = ctx // NZ, lax.rem(ctx, NZ)
    x, core = ten // 2, lax.rem(ten, 2)

    def wrap(i, n):
        return lax.rem(i + 2 * n, n)

    def at_ctx(yy, zz):
        return (wrap(yy, NY) * NZ + wrap(zz, NZ), ten)

    def at_ten(xx, cc):
        return (ctx, wrap(xx, NX) * 2 + cc)

    up, down, right, left = at_ctx(y + 1, z), at_ctx(y - 1, z), at_ctx(y, z + 1), at_ctx(y, z - 1)
    sibling, x_up, x_down = at_ten(x, 1 - core), at_ten(x + 1, core), at_ten(x - 1, core)

    barrier = pltpu.get_barrier_semaphore()
    peers = (up, down, right, left, sibling, x_up, x_down)
    for peer in peers:
        pl.semaphore_signal(barrier, inc=1, device_id=peer, device_id_type=MESH)

    w_copy = pltpu.make_async_copy(w_hbm, w, w_sem)
    w_copy.start()

    picks = picks_ref[...].reshape(1, CAP)
    count = jnp.sum(jnp.where(picks < TOK_DEV, 1.0, 0.0), axis=1, keepdims=True)
    row_id = lax.broadcasted_iota(jnp.int32, (CAP, HD), 0)
    valid = row_id.astype(jnp.float32) < count
    k_all, v_all = k_ref[...], v_ref[...]
    own[:, :HD] = jnp.where(valid, k_all.astype(jnp.float32), k_all[:1].astype(jnp.float32)).astype(jnp.bfloat16)
    own[:, HD:] = jnp.where(valid, v_all.astype(jnp.float32), FILL).astype(jnp.bfloat16)

    def place(name):
        return held.at[pl.ds(PLACE[name], ROWS[part_of(name)]), :]

    def own_part(part):
        return own.at[pl.ds(FIRST[part], ROWS[part]), :]

    def own_row(offset):
        if offset == 0:
            return own_part("A")
        name = ("ZL", "A", offset) if 0 < offset < 4 else ("ZR", "A", -offset if offset < 0 else 4)
        return place(name)

    def source(name):
        kind = name[0]
        if kind in ("ZR", "ZL"):
            _, stream, step = name
            target = right if kind == "ZR" else left
            if step > 1:
                return place((kind, stream, step - 1)), target
            if stream in ("A", "B0"):
                return own_part(stream[0]), target
            return place(("YB", {"Bm": "P", "Bp": "M", "B2": "2"}[stream])), target
        if kind == "YB":
            return (place(("YB", "P")) if name[1] == "2" else own_part("B")), (down if name[1] == "M" else up)
        if kind == "YP":
            return own_row(name[1]), up
        if kind == "YM":
            return own_row(name[1]), down
        if kind == "YP2":
            return place(("YP", name[1])), up
        return place(("YM", name[1])), down

    def shard(name):
        kind = name[0]
        if kind in ("ZR", "ZL"):
            return wrap(y + ROW_OF[name[1]], NY), wrap(z - name[2] if kind == "ZR" else z + name[2], NZ)
        if kind == "YB":
            return wrap(y + {"P": -1, "M": 1, "2": 2}[name[1]], NY), z
        return wrap(y + {"YP": -1, "YM": 1, "YP2": 2, "YM2": 2}[kind], NY), wrap(z + name[1], NZ)

    def transfer(name):
        i = NUMBER[name]
        src, target = source(name)
        return pltpu.make_async_remote_copy(
            src, place(name), send_sem.at[i], recv_sem.at[i], device_id=target, device_id_type=MESH
        )

    def start(name):
        transfer(name).start()

    def open_ring(stream):
        start(("ZR", stream, 1))
        start(("ZL", stream, 1))

    def open_column(offset):
        start(("YP", offset))
        start(("YM", offset))

    def arrive(name):
        transfer(name).wait_recv()
        kind = name[0]
        if kind in ("ZR", "ZL"):
            _, stream, step = name
            if step < TURNS[stream][0 if kind == "ZR" else 1]:
                start((kind, stream, step + 1))
            if stream == "A":
                open_column(step if kind == "ZL" else (-step if step < 4 else 4))
        elif kind == "YP" and name[1] in UPWARDS:
            start(("YP2", name[1]))
        elif kind == "YM" and name[1] not in UPWARDS:
            start(("YM2", name[1]))
        elif name == ("YB", "P"):
            start(("YB", "2"))
        for stream in OPENS.get(name, ()):
            open_ring(stream)

    def qk(g, half, keys):
        q = q_ref[half * TILE : (half + 1) * TILE, g * HD : (g + 1) * HD]
        return lax.dot_general(q, keys, (((1,), (1,)), ((), ())), preferred_element_type=jnp.float32)

    def tile(g, half):
        return pl.ds((half * GROUP + g) * TILE, TILE)

    def diagonal(half):
        if half == 0:
            va[:CAP, :HD] = v_ref[...]
            va[:CAP, HD:] = jnp.ones((CAP, HD), jnp.bfloat16)
        for g in range(GROUP):
            rows = tile(g, half)
            scores = qk(g, half, k_ref[...])
            i = lax.broadcasted_iota(jnp.int32, scores.shape, 0) + half * TILE
            j = lax.broadcasted_iota(jnp.int32, scores.shape, 1)
            scores = jnp.where(j <= i, scores, NEG)
            top = jnp.max(scores, axis=1, keepdims=True)
            weights = jnp.exp2((scores - top) * KAPPA).astype(jnp.bfloat16)
            acc[rows, :] = jnp.dot(weights, va[:CAP, :], preferred_element_type=jnp.float32)
            row_max[rows, :] = jnp.broadcast_to(top, (TILE, HD))

    def unit(u, half):
        n = UNIT_ROWS[u]
        here = pl.ds(PLACE[UNITS[u][0]], n)
        seen = []
        for name in UNITS[u]:
            yy, zz = shard(name)
            seen.append(jnp.logical_or(yy < y, jnp.logical_and(yy == y, zz < z)))
        some = seen[0]
        for other in seen[1:]:
            some = jnp.logical_or(some, other)

        @pl.when(some)
        def _():
            if half == 0:
                block = held[here, HD:]
                real = block < FILL / 2
                va[:n, :HD] = jnp.where(real, block, 0).astype(jnp.bfloat16)
                va[:n, HD:] = jnp.where(real, 1, 0).astype(jnp.bfloat16)
            column = lax.broadcasted_iota(jnp.int32, (1, n), 1)
            hide = jnp.zeros((1, n), jnp.float32)
            for name, shown in zip(UNITS[u], seen):
                first = PLACE[name] - PLACE[UNITS[u][0]]
                inside = jnp.logical_and(column >= first, column < first + ROWS[part_of(name)])
                hide = jnp.where(inside, jnp.where(shown, 0.0, NEG), hide)
            for g in range(GROUP):
                rows = tile(g, half)
                scores = qk(g, half, held[here, :HD]) + hide
                old = row_max[rows, :]
                new = jnp.maximum(old, jnp.max(scores, axis=1, keepdims=True))
                weights = jnp.exp2((scores - new[:, :1]) * KAPPA).astype(jnp.bfloat16)
                factor = jnp.exp2((old - new) * KAPPA)
                more = jnp.dot(weights, va[:n, :], preferred_element_type=jnp.float32)
                acc[rows, :HD] = acc[rows, :HD] * factor + more[:, :HD]
                acc[rows, HD:] = acc[rows, HD:] * factor + more[:, HD:]
                row_max[rows, :] = new

    def normalize(half):
        for g in range(GROUP):
            rows = tile(g, half)
            att[half * TILE : (half + 1) * TILE, g * HD : (g + 1) * HD] = (
                acc[rows, :HD] / acc[rows, HD:]
            ).astype(jnp.bfloat16)

    def block_rows(b):
        return pl.ds(b * TILE, TILE)

    def partial(d, cc, b):
        cols = pl.ds(pl.multiple_of((wrap(x + d, NX) * 2 + cc) * WIDTH, 128), WIDTH)
        return jnp.dot(att[block_rows(b), :], w[:, cols], preferred_element_type=jnp.float32)

    def to_sibling(d, b):
        i = 2 * d + b
        return pltpu.make_async_remote_copy(
            sib_out.at[d, block_rows(b)], sib_in.at[d, block_rows(b)], sib_send.at[i], sib_recv.at[i],
            device_id=sibling, device_id_type=MESH,
        )

    def x_copy(kind, way, b):
        i = (kind * 2 + way) * 2 + b
        first, count_rows = BLOCKS[b][way if kind < 2 else 1 - way]
        rows = pl.ds(first, count_rows)
        if kind == 0:
            src, dst = hop_out.at[rows], hop_in.at[rows]
        else:
            src, dst = end_out.at[way, rows], end_in.at[way, rows]
        return pltpu.make_async_remote_copy(
            src, dst, x_send.at[i], x_recv.at[i], device_id=(x_up, x_down)[way], device_id_type=MESH
        )

    def send_sibling(d, b):
        sib_out[d, block_rows(b)] = partial(d, 1 - core, b).astype(jnp.bfloat16)
        to_sibling(d, b).start()

    def chip_sum(d, b):
        mine = partial(d, core, b)
        to_sibling(d, b).wait_recv()
        return mine + sib_in[d, block_rows(b)].astype(jnp.float32)

    def far(b):
        send_sibling(2, b)
        send_sibling(1, b)
        hop_out[block_rows(b), :] = chip_sum(2, b).astype(jnp.bfloat16)
        x_copy(0, 0, b).start()
        x_copy(0, 1, b).start()
        send_sibling(3, b)

    def near(b):
        for way, d in ((0, 1), (1, 3)):
            total[way, block_rows(b)] = chip_sum(d, b)
            first, count_rows = BLOCKS[b][1 - way]
            rows = pl.ds(first, count_rows)
            end_out[way, rows] = total[way, rows].astype(jnp.bfloat16)
            x_copy(2, way, b).start()
        send_sibling(0, b)

    def pass_on(b):
        for way in (0, 1):
            first, count_rows = BLOCKS[b][way]
            rows = pl.ds(first, count_rows)
            x_copy(0, way, b).wait_recv()
            end_out[way, rows] = (total[way, rows] + hop_in[rows, :].astype(jnp.float32)).astype(jnp.bfloat16)
            x_copy(1, way, b).start()

    def finish(b):
        rows = block_rows(b)
        total[0, rows] = chip_sum(0, b)
        for way in (0, 1):
            here = pl.ds(*BLOCKS[b][way])
            x_copy(2, 1 - way, b).wait_recv()
            x_copy(1, way, b).wait_recv()
            projected = total[0, here] + end_in[0, here].astype(jnp.float32) + end_in[1, here].astype(jnp.float32)
            residual = stream_ref[here, :].astype(jnp.float32)
            inside = slice(BLOCKS[b][way][0], sum(BLOCKS[b][way]))
            updated = jnp.where(wide_valid[inside], residual + gain[inside] * projected, residual)
            out_ref[here, :] = updated.astype(jnp.bfloat16)

    pl.semaphore_wait(barrier, len(peers))
    for what in FIRST_SENDS:
        if what == "YB":
            start(("YB", "P"))
            start(("YB", "M"))
        elif what == "YA":
            open_column(0)
        else:
            open_ring(what)

    for what, *rest in ORDER[:-1]:
        if what == "w":
            arrive(tuple(rest))
        elif rest[0] == "diag":
            diagonal(rest[1])
        else:
            unit(*rest)

    normalize(0)
    w_copy.wait()
    far(0)
    unit(*ORDER[-1][1:])
    normalize(1)
    near(0)
    far(1)
    pass_on(0)
    near(1)
    pass_on(1)

    router = router_ref[...].reshape(1, CAP)
    eye = lax.broadcasted_iota(jnp.int32, (CAP, CAP), 0) == lax.broadcasted_iota(jnp.int32, (CAP, CAP), 1)
    gain = jnp.sum(jnp.where(eye, router, 0.0), axis=1, keepdims=True)
    wide_valid = lax.broadcasted_iota(jnp.int32, (CAP, WIDTH), 0).astype(jnp.float32) < count
    finish(0)
    finish(1)

    for name in G_IDS:
        transfer(name).wait_send()
    for b in (0, 1):
        for d in range(NX):
            to_sibling(d, b).wait_send()
        for kind in range(3):
            for way in (0, 1):
                x_copy(kind, way, b).wait_send()


def local(stream_rows, picks, router, queries, keys, values, out_weight):
    vmem = pl.BlockSpec(memory_space=pltpu.VMEM)
    bf16, f32 = jnp.bfloat16, jnp.float32
    dma = pltpu.SemaphoreType.DMA
    return pl.pallas_call(
        kernel,
        out_shape=jax.ShapeDtypeStruct(stream_rows.shape, bf16),
        in_specs=[vmem] * 6 + [pl.BlockSpec(memory_space=pl.ANY)],
        out_specs=vmem,
        scratch_shapes=[
            pltpu.VMEM((CAP, 2 * HD), bf16),
            pltpu.VMEM((sum(UNIT_ROWS), 2 * HD), bf16),
            pltpu.VMEM((max(UNIT_ROWS), 2 * HD), bf16),
            pltpu.VMEM((GROUP * CAP, HD), f32),
            pltpu.VMEM((GROUP * CAP, 2 * HD), f32),
            pltpu.VMEM(out_weight.shape, bf16),
            pltpu.VMEM((CAP, GROUP * HD), bf16),
            pltpu.VMEM((NX, CAP, WIDTH), bf16),
            pltpu.VMEM((NX, CAP, WIDTH), bf16),
            pltpu.VMEM((CAP, WIDTH), bf16),
            pltpu.VMEM((CAP, WIDTH), bf16),
            pltpu.VMEM((2, CAP, WIDTH), bf16),
            pltpu.VMEM((2, CAP, WIDTH), bf16),
            pltpu.VMEM((2, CAP, WIDTH), f32),
            dma((N_GATHER,)),
            dma((N_GATHER,)),
            dma((2 * NX,)),
            dma((2 * NX,)),
            dma((12,)),
            dma((12,)),
            dma,
        ],
        compiler_params=pltpu.CompilerParams(
            collective_id=0, has_side_effects=True, vmem_limit_bytes=56 * 2**20
        ),
        cost_estimate=pl.CostEstimate(flops=8 * 10**9, bytes_accessed=10**7, transcendentals=10**7),
    )(queries, keys, values, picks, router, stream_rows, out_weight)


def solution(mesh):
    placed = (
        P("context", "tensor"),
        P("context"),
        P("context"),
        P("context", "tensor"),
        P("context", "tensor"),
        P("context", "tensor"),
        P("tensor", None),
    )
    return jax.shard_map(
        local, mesh=mesh, in_specs=placed, out_specs=P("context", "tensor"), check_vma=False
    )
```

time: 81.2 us -> 77 us (0.948)
  local copies, waits for them, and re-layouts: 4.39 us -> 1.87 us
  Pallas kernels: 76.4 us -> 75 us
    reshape x2 -> x0, local copies, waits for them, and re-layouts: 2.52 us -> none  [the longest x1 1.27 us: local(): router.reshape(1, CAP)]
    pallas_call x1, Pallas kernels: 76.4 us -> 75 us  [local(): pl.pallas_call(kernel, out_shape=jax.ShapeDtypeStruct(stream_rows.shape,...]
where the time goes in v2:
time: 77 us; the launch traced here: 76.9 us
  Pallas kernels  75 us (97%)
  local copies, waits for them, and re-layouts  1.87 us (2%)
    pallas_call x1, Pallas kernels, local(): pl.pallas_call(kernel, out_shape=jax.ShapeDtypeStruct(stream_rows.shape,...  75 us
    unnamed x1, local copies, waits for them, and re-layouts  1.87 us

profile of v2, /device:TPU:25, one launch (start us, length us, event | category | flops | bytes accessed | tf_op | source)
XLA Modules:
  0.0 76.9 jit_solution(7316126123939500070)
XLA Ops:
  0.0 75.0 %shard_map.73 = bf16[288,896]{1,0:T(8,128)(2,1)} custom-call(bf16[288,512]{1,0:T(8,128)(2,1)} %q_ref.1, bf16[288,128]{1,0:T(8,128)(2,1)} %k_ref.1, bf16[288,128]{1,0:T(8,128)(2,1)} %v_ref.1, s32[288]{0:T(512)} %picks_ref.1, f32[288]{0:T(512)} %router_ref.1, bf16[288,896]{1,0:T(8,128)(2,1)} %stream_ref.1, bf16[512,7168]{1,0:T(8,128)(2,1)} %w_hbm.1), custom_call_target="tpu_custom_call" | custom-call | flops 8000000000 | bytes 10000000 | tf_op jit(solution)/shard_map/pallas_call | solution.py:394
  75.0 1.9 %copy.9 = bf16[288,896]{1,0:T(8,128)(2,1)} copy(bf16[288,896]{1,0:T(8,128)(2,1)} %shard_map.73) | data formatting | bytes 1032192

commit v3 on v2

--- a/solution.py
+++ b/solution.py
@@ -18,51 +18,47 @@
 FILL = 64.0
 TILE = 144
 
-ROWS = {"A": 176, "B": 112}
-FIRST = {"A": 0, "B": 176}
-TURNS = {"A": (4, 3), "B0": (4, 3), "Bm": (3, 4), "Bp": (3, 4), "B2": (3, 4)}
+ROWS = {"A": 192, "B": 96}
+FIRST = {"A": 0, "B": 192}
+TURNS = {"A": (4, 3), "B0": (3, 4), "Bm": (3, 4), "Bp": (3, 4), "B2": (4, 3)}
 ROW_OF = {"A": 0, "B0": 0, "Bm": 3, "Bp": 1, "B2": 2}
 OFFSETS = (0, -1, -2, -3, 4, 1, 2, 3)
 UPWARDS = (0, -1, -2, -3)
 FIRST_SENDS = ("YB", "A", "YA", "B0")
 UNITS = (
-    (("YB", "P"), ("YB", "M"), ("ZR", "A", 1), ("ZL", "A", 1),),
-    (("YP", 0), ("YM", 0), ("ZR", "B0", 1), ("ZL", "B0", 1),),
-    (("YB", "2"), ("ZR", "A", 2), ("YM", -1), ("ZL", "A", 2),),
-    (("YP", -1), ("ZR", "B0", 2), ("ZL", "B0", 2), ("YM", 1),),
-    (("YP", 1), ("ZR", "Bp", 1), ("ZL", "Bp", 1), ("ZL", "B2", 1),),
-    (("YM", -2), ("YP2", 0), ("ZR", "A", 3),),
-    (("ZR", "B2", 1), ("ZL", "A", 3), ("YM", 2), ("YP", -2), ("ZR", "Bm", 1),),
-    (("ZL", "Bm", 1), ("YM2", 1), ("ZR", "B0", 3), ("ZL", "B0", 3),),
-    (("YP", 2), ("ZR", "Bp", 2), ("ZL", "Bp", 2), ("YM", -3), ("YP2", -1),),
-    (("ZL", "B2", 2), ("ZR", "A", 4), ("ZL", "Bm", 2), ("YM", 3), ("YP", -3),),
-    (("ZR", "B2", 2), ("ZL", "Bp", 3), ("ZR", "Bm", 2), ("YM2", 2),),
-    (("YP", 3), ("ZL", "B2", 3), ("ZR", "B0", 4), ("YM", 4), ("ZL", "Bm", 3), ("YP2", -2), ("ZR", "Bp", 3),),
-    (("ZL", "Bp", 4), ("ZR", "B2", 3), ("YM2", 3), ("YP", 4), ("ZL", "B2", 4),),
-    (("ZR", "Bm", 3), ("ZL", "Bm", 4), ("YP2", -3), ("YM2", 4),),
+    (("ZR", "A", 1), ("ZL", "A", 1), ("YB", "P"), ("YB", "M"), ("ZR", "B0", 1), ("ZL", "B0", 1),),
+    (("YP", 0), ("YM", 0), ("ZR", "A", 2), ("YB", "2"), ("ZR", "Bm", 1),),
+    (("YP", -1), ("YM", -1), ("ZL", "Bm", 1), ("ZR", "B0", 2), ("ZL", "B0", 2), ("ZR", "Bm", 2),),
+    (("ZL", "A", 2), ("YP", 1), ("YM", 1), ("YP2", 0),),
+    (("ZR", "A", 3), ("YM", -2), ("ZL", "Bm", 2), ("ZR", "B0", 3), ("ZL", "Bp", 1), ("ZR", "Bp", 1),),
+    (("ZL", "A", 3), ("YP", -2), ("ZL", "B0", 3), ("ZR", "Bm", 3), ("ZL", "Bm", 3), ("ZR", "B2", 1),),
+    (("YM", 2), ("YP2", -1), ("YM2", 1), ("ZL", "B2", 1), ("ZL", "Bp", 2),),
+    (("YP", 2), ("YM", -3), ("ZL", "B0", 4), ("ZR", "Bp", 2), ("ZL", "Bm", 4), ("ZR", "B2", 2),),
+    (("ZR", "A", 4), ("YP", -3), ("YM", 3), ("ZL", "B2", 2), ("ZL", "Bp", 3),),
+    (("YP", 3), ("YM2", 2), ("YP2", -2), ("ZR", "Bp", 3), ("ZR", "B2", 3),),
+    (("YM", 4), ("YP", 4), ("YM2", 3), ("ZL", "B2", 3), ("ZL", "Bp", 4),),
+    (("YP2", -3), ("YM2", 4), ("ZR", "B2", 4),),
 )
 ORDER = (
-    ("c", "diag", 0), ("c", "diag", 1), ("w", "YB", "P"), ("w", "YB", "M"), ("w", "ZR", "A", 1), ("w", "ZL", "A", 1),
-    ("c", 0, 0), ("c", 0, 1), ("w", "YP", 0), ("w", "YM", 0), ("w", "ZR", "B0", 1), ("w", "ZL", "B0", 1),
-    ("c", 1, 0), ("c", 1, 1), ("w", "YB", "2"), ("w", "ZR", "A", 2), ("w", "YM", -1), ("w", "ZL", "A", 2),
-    ("c", 2, 0), ("w", "YP", -1), ("c", 2, 1), ("w", "ZR", "B0", 2), ("w", "ZL", "B0", 2), ("w", "YM", 1),
-    ("c", 3, 0), ("w", "YP", 1), ("w", "ZR", "Bp", 1), ("w", "ZL", "Bp", 1), ("c", 3, 1), ("w", "ZL", "B2", 1),
-    ("c", 4, 0), ("w", "YM", -2), ("w", "YP2", 0), ("w", "ZR", "A", 3), ("c", 4, 1), ("c", 5, 0),
-    ("w", "ZR", "B2", 1), ("w", "ZL", "A", 3), ("w", "YM", 2), ("c", 5, 1), ("w", "YP", -2), ("w", "ZR", "Bm", 1),
-    ("w", "ZL", "Bm", 1), ("c", 6, 0), ("w", "YM2", 1), ("w", "ZR", "B0", 3), ("w", "ZL", "B0", 3), ("w", "YP", 2),
-    ("c", 6, 1), ("c", 7, 0), ("w", "ZR", "Bp", 2), ("w", "ZL", "Bp", 2), ("c", 7, 1), ("w", "YM", -3),
-    ("w", "YP2", -1), ("w", "ZL", "B2", 2), ("c", 8, 0), ("w", "ZR", "A", 4), ("c", 8, 1), ("w", "ZL", "Bm", 2),
-    ("w", "YM", 3), ("w", "YP", -3), ("w", "ZR", "B2", 2), ("c", 9, 0), ("w", "ZL", "Bp", 3), ("c", 9, 1),
-    ("w", "ZR", "Bm", 2), ("w", "YM2", 2), ("w", "YP", 3), ("w", "ZL", "B2", 3), ("c", 10, 0), ("w", "ZR", "B0", 4),
-    ("c", 10, 1), ("w", "YM", 4), ("w", "ZL", "Bm", 3), ("w", "YP2", -2), ("w", "ZR", "Bp", 3), ("c", 11, 0),
-    ("w", "ZL", "Bp", 4), ("w", "ZR", "B2", 3), ("c", 11, 1), ("w", "YM2", 3), ("w", "YP", 4), ("w", "ZL", "B2", 4),
-    ("w", "ZR", "Bm", 3), ("c", 12, 0), ("w", "ZL", "Bm", 4), ("c", 12, 1), ("w", "YP2", -3), ("w", "YM2", 4),
-    ("c", 13, 0), ("c", 13, 1),
+    ("c", "diag"), ("w", "YB", "P"), ("w", "YB", "M"), ("w", "ZR", "A", 1), ("w", "ZL", "A", 1),
+    ("w", "YP", 0), ("w", "YM", 0), ("w", "ZR", "B0", 1), ("w", "ZL", "B0", 1), ("c", 0), ("w", "YB", "2"),
+    ("w", "ZR", "Bm", 1), ("w", "ZL", "Bm", 1), ("w", "ZR", "A", 2), ("w", "YP", -1), ("w", "YM", -1),
+    ("w", "ZL", "A", 2), ("c", 1), ("w", "ZR", "B0", 2), ("w", "ZL", "B0", 2), ("w", "YP", 1), ("w", "YM", 1),
+    ("w", "ZR", "Bm", 2), ("w", "ZL", "Bm", 2), ("c", 2), ("w", "YP2", 0), ("c", 3), ("w", "ZR", "A", 3),
+    ("w", "YM", -2), ("w", "ZL", "A", 3), ("w", "ZR", "B0", 3), ("w", "ZL", "Bp", 1), ("w", "YP", -2),
+    ("w", "YM", 2), ("w", "ZR", "Bp", 1), ("c", 4), ("w", "ZL", "B0", 3), ("w", "ZR", "Bm", 3),
+    ("w", "ZL", "Bm", 3), ("w", "YP2", -1), ("w", "YM2", 1), ("w", "ZR", "B2", 1), ("w", "ZL", "B2", 1), ("c", 5),
+    ("w", "ZL", "Bp", 2), ("w", "YP", 2), ("w", "YM", -3), ("w", "ZR", "A", 4), ("c", 6), ("w", "ZL", "B0", 4),
+    ("w", "ZR", "Bp", 2), ("w", "YP", -3), ("w", "ZL", "Bm", 4), ("w", "YM", 3), ("w", "ZR", "B2", 2), ("c", 7),
+    ("w", "ZL", "B2", 2), ("w", "YP", 3), ("w", "ZL", "Bp", 3), ("w", "YM2", 2), ("c", 8), ("w", "ZR", "Bp", 3),
+    ("w", "YP2", -2), ("w", "YM", 4), ("w", "ZR", "B2", 3), ("c", 9), ("w", "ZL", "B2", 3), ("w", "YP", 4),
+    ("w", "YM2", 3), ("w", "ZL", "Bp", 4), ("c", 10), ("w", "ZR", "B2", 4), ("w", "YP2", -3), ("w", "YM2", 4),
+    ("c", 11),
 )
 OPENS = {
-    ("ZL", "B0", 1): ("Bp",),
-    ("ZR", "A", 2): ("B2",),
-    ("ZL", "A", 2): ("Bm",),
+    ("YB", "P"): ("Bm",),
+    ("ZR", "B0", 2): ("Bp",),
+    ("ZL", "Bm", 2): ("B2",),
 }
 
 Z_IDS = [(side, s, i + 1) for s, (r, l) in TURNS.items() for side, n in (("ZR", r), ("ZL", l)) for i in range(n)]
@@ -210,11 +206,10 @@
     def tile(g, half):
         return pl.ds((half * GROUP + g) * TILE, TILE)
 
-    def diagonal(half):
-        if half == 0:
-            va[:CAP, :HD] = v_ref[...]
-            va[:CAP, HD:] = jnp.ones((CAP, HD), jnp.bfloat16)
-        for g in range(GROUP):
+    def diagonal():
+        va[:CAP, :HD] = v_ref[...]
+        va[:CAP, HD:] = jnp.ones((CAP, HD), jnp.bfloat16)
+        for half, g in ((0, 0), (0, 1), (0, 2), (0, 3), (1, 0), (1, 1), (1, 2), (1, 3)):
             rows = tile(g, half)
             scores = qk(g, half, k_ref[...])
             i = lax.broadcasted_iota(jnp.int32, scores.shape, 0) + half * TILE
@@ -225,7 +220,7 @@
             acc[rows, :] = jnp.dot(weights, va[:CAP, :], preferred_element_type=jnp.float32)
             row_max[rows, :] = jnp.broadcast_to(top, (TILE, HD))
 
-    def unit(u, half):
+    def unit(u, halves=(0, 1)):
         n = UNIT_ROWS[u]
         here = pl.ds(PLACE[UNITS[u][0]], n)
         seen = []
@@ -238,7 +233,7 @@
 
         @pl.when(some)
         def _():
-            if half == 0:
+            if 0 in halves:
                 block = held[here, HD:]
                 real = block < FILL / 2
                 va[:n, :HD] = jnp.where(real, block, 0).astype(jnp.bfloat16)
@@ -249,7 +244,7 @@
                 first = PLACE[name] - PLACE[UNITS[u][0]]
                 inside = jnp.logical_and(column >= first, column < first + ROWS[part_of(name)])
                 hide = jnp.where(inside, jnp.where(shown, 0.0, NEG), hide)
-            for g in range(GROUP):
+            for half, g in ((h, g) for h in halves for g in range(GROUP)):
                 rows = tile(g, half)
                 scores = qk(g, half, held[here, :HD]) + hide
                 old = row_max[rows, :]
@@ -355,14 +350,15 @@
         if what == "w":
             arrive(tuple(rest))
         elif rest[0] == "diag":
-            diagonal(rest[1])
+            diagonal()
         else:
-            unit(*rest)
-
+            unit(rest[0])
+
+    unit(ORDER[-1][1], (0,))
     normalize(0)
     w_copy.wait()
     far(0)
-    unit(*ORDER[-1][1:])
+    unit(ORDER[-1][1], (1,))
     normalize(1)
     near(0)
     far(1)

time: 77 us -> 65.9 us (0.86)
  Pallas kernels: 75 us -> 63.8 us
    pallas_call x1, Pallas kernels: 75 us -> 63.8 us  [local(): pl.pallas_call(kernel, out_shape=jax.ShapeDtypeStruct(stream_rows.shape,...]
where the time goes in v3:
time: 65.9 us; the launch traced here: 65.6 us
  Pallas kernels  63.8 us (97%)
  local copies, waits for them, and re-layouts  1.87 us (3%)
    pallas_call x1, Pallas kernels, local(): pl.pallas_call(kernel, out_shape=jax.ShapeDtypeStruct(stream_rows.shape,...  63.8 us
    unnamed x1, local copies, waits for them, and re-layouts  1.87 us

profile of v3, /device:TPU:25, one launch (start us, length us, event | category | flops | bytes accessed | tf_op | source)
XLA Modules:
  0.0 65.6 jit_solution(2161964972368268582)
XLA Ops:
  0.0 63.8 %shard_map.73 = bf16[288,896]{1,0:T(8,128)(2,1)} custom-call(bf16[288,512]{1,0:T(8,128)(2,1)} %q_ref.1, bf16[288,128]{1,0:T(8,128)(2,1)} %k_ref.1, bf16[288,128]{1,0:T(8,128)(2,1)} %v_ref.1, s32[288]{0:T(512)} %picks_ref.1, f32[288]{0:T(512)} %router_ref.1, bf16[288,896]{1,0:T(8,128)(2,1)} %stream_ref.1, bf16[512,7168]{1,0:T(8,128)(2,1)} %w_hbm.1), custom_call_target="tpu_custom_call" | custom-call | flops 8000000000 | bytes 10000000 | tf_op jit(solution)/shard_map/pallas_call | solution.py:390
  63.8 1.9 %copy.9 = bf16[288,896]{1,0:T(8,128)(2,1)} copy(bf16[288,896]{1,0:T(8,128)(2,1)} %shard_map.73) | data formatting | bytes 1032192

commit v4 on v3

--- a/solution.py
+++ b/solution.py
@@ -17,48 +17,52 @@
 NEG = -1e30
 FILL = 64.0
 TILE = 144
-
-ROWS = {"A": 192, "B": 96}
-FIRST = {"A": 0, "B": 192}
-TURNS = {"A": (4, 3), "B0": (3, 4), "Bm": (3, 4), "Bp": (3, 4), "B2": (4, 3)}
+VROWS = 144
+ALL_COLS = ((0, 384), (384, 384), (768, 384))
+LOW_COLS = ((0, 384), (384, 256))
+HIGH_COLS = ((640, 512),)
+
+ROWS = {"A": 176, "B": 112}
+FIRST = {"A": 0, "B": 176}
+TURNS = {"A": (4, 3), "B0": (4, 3), "Bm": (3, 4), "Bp": (3, 4), "B2": (3, 4)}
 ROW_OF = {"A": 0, "B0": 0, "Bm": 3, "Bp": 1, "B2": 2}
 OFFSETS = (0, -1, -2, -3, 4, 1, 2, 3)
 UPWARDS = (0, -1, -2, -3)
-FIRST_SENDS = ("YB", "A", "YA", "B0")
+FIRST_SENDS = ("A", "YB", "YA", "B0")
 UNITS = (
-    (("ZR", "A", 1), ("ZL", "A", 1), ("YB", "P"), ("YB", "M"), ("ZR", "B0", 1), ("ZL", "B0", 1),),
-    (("YP", 0), ("YM", 0), ("ZR", "A", 2), ("YB", "2"), ("ZR", "Bm", 1),),
-    (("YP", -1), ("YM", -1), ("ZL", "Bm", 1), ("ZR", "B0", 2), ("ZL", "B0", 2), ("ZR", "Bm", 2),),
-    (("ZL", "A", 2), ("YP", 1), ("YM", 1), ("YP2", 0),),
-    (("ZR", "A", 3), ("YM", -2), ("ZL", "Bm", 2), ("ZR", "B0", 3), ("ZL", "Bp", 1), ("ZR", "Bp", 1),),
-    (("ZL", "A", 3), ("YP", -2), ("ZL", "B0", 3), ("ZR", "Bm", 3), ("ZL", "Bm", 3), ("ZR", "B2", 1),),
-    (("YM", 2), ("YP2", -1), ("YM2", 1), ("ZL", "B2", 1), ("ZL", "Bp", 2),),
-    (("YP", 2), ("YM", -3), ("ZL", "B0", 4), ("ZR", "Bp", 2), ("ZL", "Bm", 4), ("ZR", "B2", 2),),
-    (("ZR", "A", 4), ("YP", -3), ("YM", 3), ("ZL", "B2", 2), ("ZL", "Bp", 3),),
-    (("YP", 3), ("YM2", 2), ("YP2", -2), ("ZR", "Bp", 3), ("ZR", "B2", 3),),
-    (("YM", 4), ("YP", 4), ("YM2", 3), ("ZL", "B2", 3), ("ZL", "Bp", 4),),
-    (("YP2", -3), ("YM2", 4), ("ZR", "B2", 4),),
+    (("ZR", "A", 1), ("ZL", "A", 1), ("YP", 0), ("YB", "P"), ("YB", "M"), ("ZR", "B0", 1), ("ZL", "B0", 1),),
+    (("YM", 0), ("ZR", "A", 2), ("YM", -1), ("ZL", "A", 2),),
+    (("YP", -1), ("YM", 1), ("YP", 1), ("YB", "2"), ("ZR", "B0", 2),),
+    (("YP2", 0), ("ZR", "A", 3), ("YM", -2), ("ZL", "B0", 2), ("ZL", "Bm", 1),),
+    (("ZL", "A", 3), ("YP", -2), ("YM", 2), ("ZR", "Bm", 1), ("ZR", "Bp", 1),),
+    (("YP", 2), ("ZL", "Bp", 1), ("ZR", "B0", 3), ("ZL", "B0", 3), ("ZR", "B2", 1), ("ZL", "B2", 1),),
+    (("YM2", 1), ("YP2", -1), ("YM", -3), ("ZL", "Bm", 2), ("ZL", "Bp", 2),),
+    (("ZR", "A", 4), ("YP", -3), ("YM", 3), ("YP", 3), ("YM2", 2), ("ZR", "Bm", 2),),
+    (("YP2", -2), ("YM", 4), ("ZL", "B2", 2), ("ZR", "Bp", 2), ("ZR", "B0", 4), ("ZL", "Bm", 3), ("ZR", "B2", 2), ("ZL", "Bp", 3),),
+    (("YP", 4), ("YM2", 3), ("YP2", -3), ("ZR", "Bm", 3), ("ZL", "B2", 3),),
+    (("YM2", 4), ("ZR", "Bp", 3), ("ZL", "Bm", 4), ("ZR", "B2", 3),),
+    (("ZL", "Bp", 4), ("ZL", "B2", 4),),
 )
 ORDER = (
     ("c", "diag"), ("w", "YB", "P"), ("w", "YB", "M"), ("w", "ZR", "A", 1), ("w", "ZL", "A", 1),
     ("w", "YP", 0), ("w", "YM", 0), ("w", "ZR", "B0", 1), ("w", "ZL", "B0", 1), ("c", 0), ("w", "YB", "2"),
-    ("w", "ZR", "Bm", 1), ("w", "ZL", "Bm", 1), ("w", "ZR", "A", 2), ("w", "YP", -1), ("w", "YM", -1),
-    ("w", "ZL", "A", 2), ("c", 1), ("w", "ZR", "B0", 2), ("w", "ZL", "B0", 2), ("w", "YP", 1), ("w", "YM", 1),
-    ("w", "ZR", "Bm", 2), ("w", "ZL", "Bm", 2), ("c", 2), ("w", "YP2", 0), ("c", 3), ("w", "ZR", "A", 3),
-    ("w", "YM", -2), ("w", "ZL", "A", 3), ("w", "ZR", "B0", 3), ("w", "ZL", "Bp", 1), ("w", "YP", -2),
-    ("w", "YM", 2), ("w", "ZR", "Bp", 1), ("c", 4), ("w", "ZL", "B0", 3), ("w", "ZR", "Bm", 3),
-    ("w", "ZL", "Bm", 3), ("w", "YP2", -1), ("w", "YM2", 1), ("w", "ZR", "B2", 1), ("w", "ZL", "B2", 1), ("c", 5),
-    ("w", "ZL", "Bp", 2), ("w", "YP", 2), ("w", "YM", -3), ("w", "ZR", "A", 4), ("c", 6), ("w", "ZL", "B0", 4),
-    ("w", "ZR", "Bp", 2), ("w", "YP", -3), ("w", "ZL", "Bm", 4), ("w", "YM", 3), ("w", "ZR", "B2", 2), ("c", 7),
-    ("w", "ZL", "B2", 2), ("w", "YP", 3), ("w", "ZL", "Bp", 3), ("w", "YM2", 2), ("c", 8), ("w", "ZR", "Bp", 3),
-    ("w", "YP2", -2), ("w", "YM", 4), ("w", "ZR", "B2", 3), ("c", 9), ("w", "ZL", "B2", 3), ("w", "YP", 4),
-    ("w", "YM2", 3), ("w", "ZL", "Bp", 4), ("c", 10), ("w", "ZR", "B2", 4), ("w", "YP2", -3), ("w", "YM2", 4),
-    ("c", 11),
+    ("w", "ZR", "A", 2), ("w", "YM", -1), ("w", "ZL", "A", 2), ("c", 1), ("w", "YP", -1), ("w", "ZR", "B0", 2),
+    ("w", "ZL", "B0", 2), ("w", "YM", 1), ("w", "YP", 1), ("c", 2), ("w", "ZL", "Bm", 1), ("w", "YP2", 0),
+    ("w", "ZR", "A", 3), ("w", "YM", -2), ("c", 3), ("w", "ZR", "Bm", 1), ("w", "ZL", "A", 3), ("w", "YP", -2),
+    ("w", "YM", 2), ("w", "ZR", "Bp", 1), ("w", "ZL", "Bp", 1), ("c", 4), ("w", "ZR", "B0", 3),
+    ("w", "ZL", "B0", 3), ("w", "YP", 2), ("w", "YM2", 1), ("w", "ZR", "B2", 1), ("w", "ZL", "B2", 1), ("c", 5),
+    ("w", "YP2", -1), ("w", "YM", -3), ("w", "ZL", "Bm", 2), ("w", "ZR", "A", 4), ("w", "ZL", "Bp", 2), ("c", 6),
+    ("w", "YP", -3), ("w", "YM", 3), ("w", "ZR", "Bm", 2), ("w", "ZL", "B2", 2), ("w", "ZR", "Bp", 2),
+    ("w", "YP", 3), ("w", "YM2", 2), ("c", 7), ("w", "ZR", "B0", 4), ("w", "ZL", "Bm", 3), ("w", "YP2", -2),
+    ("w", "YM", 4), ("w", "ZR", "B2", 2), ("w", "ZL", "Bp", 3), ("c", 8), ("w", "ZR", "Bm", 3),
+    ("w", "ZL", "B2", 3), ("w", "YP", 4), ("w", "YM2", 3), ("w", "ZR", "Bp", 3), ("w", "YP2", -3), ("c", 9),
+    ("w", "ZL", "Bm", 4), ("w", "ZR", "B2", 3), ("w", "YM2", 4), ("w", "ZL", "Bp", 4), ("c", 10),
+    ("w", "ZL", "B2", 4), ("c", 11),
 )
 OPENS = {
-    ("YB", "P"): ("Bm",),
-    ("ZR", "B0", 2): ("Bp",),
-    ("ZL", "Bm", 2): ("B2",),
+    ("ZR", "A", 2): ("Bm",),
+    ("ZL", "A", 2): ("Bp",),
+    ("ZL", "B0", 2): ("B2",),
 }
 
 Z_IDS = [(side, s, i + 1) for s, (r, l) in TURNS.items() for side, n in (("ZR", r), ("ZL", l)) for i in range(n)]
@@ -88,7 +92,7 @@
 
 def kernel(
     q_ref, k_ref, v_ref, picks_ref, router_ref, stream_ref, w_hbm, out_ref,
-    own, held, va, row_max, acc, w, att, sib_out, sib_in, hop_out, hop_in, end_out, end_in, total,
+    own, held, stacked, vt, top, acc, w, att, sib_out, sib_in, hop_out, hop_in, end_out, end_in, total,
     send_sem, recv_sem, sib_send, sib_recv, x_send, x_recv, w_sem,
 ):
     ctx, ten = lax.axis_index("context"), lax.axis_index("tensor")
@@ -199,28 +203,35 @@
         for stream in OPENS.get(name, ()):
             open_ring(stream)
 
-    def qk(g, half, keys):
-        q = q_ref[half * TILE : (half + 1) * TILE, g * HD : (g + 1) * HD]
-        return lax.dot_general(q, keys, (((1,), (1,)), ((), ())), preferred_element_type=jnp.float32)
-
     def tile(g, half):
         return pl.ds((half * GROUP + g) * TILE, TILE)
 
+    def stack_queries():
+        for half in (0, 1):
+            for g in range(GROUP):
+                stacked[tile(g, half), :] = q_ref[half * TILE : (half + 1) * TILE, g * HD : (g + 1) * HD]
+
+    def qk(keys, cols):
+        return lax.dot_general(
+            keys, stacked[cols, :], (((1,), (1,)), ((), ())), preferred_element_type=jnp.float32
+        )
+
     def diagonal():
-        va[:CAP, :HD] = v_ref[...]
-        va[:CAP, HD:] = jnp.ones((CAP, HD), jnp.bfloat16)
-        for half, g in ((0, 0), (0, 1), (0, 2), (0, 3), (1, 0), (1, 1), (1, 2), (1, 3)):
-            rows = tile(g, half)
-            scores = qk(g, half, k_ref[...])
-            i = lax.broadcasted_iota(jnp.int32, scores.shape, 0) + half * TILE
-            j = lax.broadcasted_iota(jnp.int32, scores.shape, 1)
+        vt[:HD, :CAP] = jnp.transpose(v_ref[...])
+        vt[HD:, :CAP] = jnp.ones((VROWS - HD, CAP), jnp.bfloat16)
+        for first, width in ALL_COLS:
+            cols = pl.ds(first, width)
+            scores = qk(k_ref[...], cols)
+            c = lax.broadcasted_iota(jnp.int32, (1, width), 1) + first
+            i = jnp.where(c >= GROUP * TILE, TILE, 0) + lax.rem(c, TILE)
+            j = lax.broadcasted_iota(jnp.int32, scores.shape, 0)
             scores = jnp.where(j <= i, scores, NEG)
-            top = jnp.max(scores, axis=1, keepdims=True)
-            weights = jnp.exp2((scores - top) * KAPPA).astype(jnp.bfloat16)
-            acc[rows, :] = jnp.dot(weights, va[:CAP, :], preferred_element_type=jnp.float32)
-            row_max[rows, :] = jnp.broadcast_to(top, (TILE, HD))
-
-    def unit(u, halves=(0, 1)):
+            high = jnp.max(scores, axis=0, keepdims=True)
+            weights = jnp.exp2((scores - high) * KAPPA).astype(jnp.bfloat16)
+            acc[:, cols] = jnp.dot(vt[:, :CAP], weights, preferred_element_type=jnp.float32)
+            top[:, cols] = jnp.broadcast_to(high, (8, width))
+
+    def unit(u, columns=ALL_COLS, fill=True):
         n = UNIT_ROWS[u]
         here = pl.ds(PLACE[UNITS[u][0]], n)
         seen = []
@@ -233,35 +244,49 @@
 
         @pl.when(some)
         def _():
-            if 0 in halves:
-                block = held[here, HD:]
+            if fill:
+                block = jnp.transpose(held[here, HD:])
                 real = block < FILL / 2
-                va[:n, :HD] = jnp.where(real, block, 0).astype(jnp.bfloat16)
-                va[:n, HD:] = jnp.where(real, 1, 0).astype(jnp.bfloat16)
-            column = lax.broadcasted_iota(jnp.int32, (1, n), 1)
-            hide = jnp.zeros((1, n), jnp.float32)
-            for name, shown in zip(UNITS[u], seen):
-                first = PLACE[name] - PLACE[UNITS[u][0]]
-                inside = jnp.logical_and(column >= first, column < first + ROWS[part_of(name)])
-                hide = jnp.where(inside, jnp.where(shown, 0.0, NEG), hide)
-            for half, g in ((h, g) for h in halves for g in range(GROUP)):
-                rows = tile(g, half)
-                scores = qk(g, half, held[here, :HD]) + hide
-                old = row_max[rows, :]
-                new = jnp.maximum(old, jnp.max(scores, axis=1, keepdims=True))
-                weights = jnp.exp2((scores - new[:, :1]) * KAPPA).astype(jnp.bfloat16)
-                factor = jnp.exp2((old - new) * KAPPA)
-                more = jnp.dot(weights, va[:n, :], preferred_element_type=jnp.float32)
-                acc[rows, :HD] = acc[rows, :HD] * factor + more[:, :HD]
-                acc[rows, HD:] = acc[rows, HD:] * factor + more[:, HD:]
-                row_max[rows, :] = new
+                vt[:HD, :n] = jnp.where(real, block, 0).astype(jnp.bfloat16)
+                vt[HD:, :n] = jnp.where(real[: VROWS - HD], 1, 0).astype(jnp.bfloat16)
+            hide = [jnp.where(shown, 0.0, NEG) for shown in seen]
+
+            def score(cols):
+                raw = qk(held[here, :HD], cols)
+                parts, first = [], 0
+                for name, shift in zip(UNITS[u], hide):
+                    rows = ROWS[part_of(name)]
+                    parts.append(raw[first : first + rows] + shift)
+                    first += rows
+                return jnp.concatenate(parts, axis=0)
+
+            def soften(cols, scores):
+                old = top[:, cols]
+                new = jnp.maximum(old, jnp.max(scores, axis=0, keepdims=True))
+                top[:, cols] = new
+                return jnp.exp2((scores - new[:1]) * KAPPA).astype(jnp.bfloat16), jnp.exp2((old - new) * KAPPA)
+
+            def mix(cols, weights, factor):
+                more = jnp.dot(vt[:, :n], weights, preferred_element_type=jnp.float32)
+                acc[:, cols] = acc[:, cols] * factor[:1] + more
+
+            spans = [pl.ds(*span) for span in columns]
+            scores, waiting = score(spans[0]), None
+            for at, cols in enumerate(spans):
+                following = score(spans[at + 1]) if at + 1 < len(spans) else None
+                softened = soften(cols, scores)
+                if waiting is not None:
+                    mix(*waiting)
+                waiting, scores = (cols, *softened), following
+            mix(*waiting)
 
     def normalize(half):
+        first, width = ((0, 640), (512, 640))[half]
+        cols = pl.ds(first, width)
+        flat = jnp.transpose(acc[:HD, cols] / acc[HD : HD + 1, cols]).astype(jnp.bfloat16)
         for g in range(GROUP):
-            rows = tile(g, half)
-            att[half * TILE : (half + 1) * TILE, g * HD : (g + 1) * HD] = (
-                acc[rows, :HD] / acc[rows, HD:]
-            ).astype(jnp.bfloat16)
+            start_row = (half * GROUP + g) * TILE - first
+            att[half * TILE : (half + 1) * TILE, g * HD : (g + 1) * HD] = flat[start_row : start_row + TILE]
 
     def block_rows(b):
         return pl.ds(b * TILE, TILE)
@@ -336,6 +361,7 @@
             updated = jnp.where(wide_valid[inside], residual + gain[inside] * projected, residual)
             out_ref[here, :] = updated.astype(jnp.bfloat16)
 
+    stack_queries()
     pl.semaphore_wait(barrier, len(peers))
     for what in FIRST_SENDS:
         if what == "YB":
@@ -354,11 +380,11 @@
         else:
             unit(rest[0])
 
-    unit(ORDER[-1][1], (0,))
+    unit(ORDER[-1][1], LOW_COLS)
     normalize(0)
     w_copy.wait()
     far(0)
-    unit(ORDER[-1][1], (1,))
+    unit(ORDER[-1][1], HIGH_COLS, False)
     normalize(1)
     near(0)
     far(1)
@@ -370,14 +396,14 @@
     eye = lax.broadcasted_iota(jnp.int32, (CAP, CAP), 0) == lax.broadcasted_iota(jnp.int32, (CAP, CAP), 1)
     gain = jnp.sum(jnp.where(eye, router, 0.0), axis=1, keepdims=True)
     wide_valid = lax.broadcasted_iota(jnp.int32, (CAP, WIDTH), 0).astype(jnp.float32) < count
-    finish(0)
-    finish(1)
-
     for name in G_IDS:
         transfer(name).wait_send()
     for b in (0, 1):
         for d in range(NX):
             to_sibling(d, b).wait_send()
+    finish(0)
+    finish(1)
+    for b in (0, 1):
         for kind in range(3):
             for way in (0, 1):
                 x_copy(kind, way, b).wait_send()
@@ -395,9 +421,10 @@
         scratch_shapes=[
             pltpu.VMEM((CAP, 2 * HD), bf16),
             pltpu.VMEM((sum(UNIT_ROWS), 2 * HD), bf16),
-            pltpu.VMEM((max(UNIT_ROWS), 2 * HD), bf16),
-            pltpu.VMEM((GROUP * CAP, HD), f32),
-            pltpu.VMEM((GROUP * CAP, 2 * HD), f32),
+            pltpu.VMEM((GROUP * CAP, HD), bf16),
+            pltpu.VMEM((VROWS, max(UNIT_ROWS)), bf16),
+            pltpu.VMEM((8, GROUP * CAP), f32),
+            pltpu.VMEM((VROWS, GROUP * CAP), f32),
             pltpu.VMEM(out_weight.shape, bf16),
             pltpu.VMEM((CAP, GROUP * HD), bf16),
             pltpu.VMEM((NX, CAP, WIDTH), bf16),

time: 65.9 us -> 64.8 us (0.983)
  Pallas kernels: 63.8 us -> 62.6 us
    pallas_call x1, Pallas kernels: 63.8 us -> 62.6 us  [local(): pl.pallas_call(kernel, out_shape=jax.ShapeDtypeStruct(stream_rows.shape,...]
where the time goes in v4:
time: 64.8 us; the launch traced here: 64.5 us
  Pallas kernels  62.6 us (97%)
  local copies, waits for them, and re-layouts  1.87 us (3%)
    pallas_call x1, Pallas kernels, local(): pl.pallas_call(kernel, out_shape=jax.ShapeDtypeStruct(stream_rows.shape,...  62.6 us
    unnamed x1, local copies, waits for them, and re-layouts  1.87 us

profile of v4, /device:TPU:25, one launch (start us, length us, event | category | flops | bytes accessed | tf_op | source)
XLA Modules:
  0.0 64.5 jit_solution(8967021572028012072)
XLA Ops:
  0.0 62.6 %shard_map.73 = bf16[288,896]{1,0:T(8,128)(2,1)} custom-call(bf16[288,512]{1,0:T(8,128)(2,1)} %q_ref.1, bf16[288,128]{1,0:T(8,128)(2,1)} %k_ref.1, bf16[288,128]{1,0:T(8,128)(2,1)} %v_ref.1, s32[288]{0:T(512)} %picks_ref.1, f32[288]{0:T(512)} %router_ref.1, bf16[288,896]{1,0:T(8,128)(2,1)} %stream_ref.1, bf16[512,7168]{1,0:T(8,128)(2,1)} %w_hbm.1), custom_call_target="tpu_custom_call" | custom-call | flops 8000000000 | bytes 10000000 | tf_op jit(solution)/shard_map/pallas_call | solution.py:416
  62.6 1.9 %copy.9 = bf16[288,896]{1,0:T(8,128)(2,1)} copy(bf16[288,896]{1,0:T(8,128)(2,1)} %shard_map.73) | data formatting | bytes 1032192

commit v5 on v4

--- a/solution.py
+++ b/solution.py
@@ -91,9 +91,9 @@
 
 
 def kernel(
-    q_ref, k_ref, v_ref, picks_ref, router_ref, stream_ref, w_hbm, out_ref,
+    q_hbm, k_ref, v_ref, picks_ref, router_ref, stream_hbm, w_hbm, out_hbm, q_ref, stream_ref, out_ref,
     own, held, stacked, vt, top, acc, w, att, sib_out, sib_in, hop_out, hop_in, end_out, end_in, total,
-    send_sem, recv_sem, sib_send, sib_recv, x_send, x_recv, w_sem,
+    send_sem, recv_sem, sib_send, sib_recv, x_send, x_recv, w_sem, in_sems, out_sems,
 ):
     ctx, ten = lax.axis_index("context"), lax.axis_index("tensor")
     y, z = ctx // NZ, lax.rem(ctx, NZ)
@@ -117,6 +117,10 @@
         pl.semaphore_signal(barrier, inc=1, device_id=peer, device_id_type=MESH)
 
     w_copy = pltpu.make_async_copy(w_hbm, w, w_sem)
+    q_copy = pltpu.make_async_copy(q_hbm, q_ref, in_sems.at[0])
+    stream_copy = pltpu.make_async_copy(stream_hbm, stream_ref, in_sems.at[1])
+    q_copy.start()
+    stream_copy.start()
     w_copy.start()
 
     picks = picks_ref[...].reshape(1, CAP)
@@ -348,6 +352,10 @@
             end_out[way, rows] = (total[way, rows] + hop_in[rows, :].astype(jnp.float32)).astype(jnp.bfloat16)
             x_copy(1, way, b).start()
 
+    def out_copy(b, way):
+        here = pl.ds(*BLOCKS[b][way])
+        return pltpu.make_async_copy(out_ref.at[here], out_hbm.at[here], out_sems.at[2 * b + way])
+
     def finish(b):
         rows = block_rows(b)
         total[0, rows] = chip_sum(0, b)
@@ -360,7 +368,9 @@
             inside = slice(BLOCKS[b][way][0], sum(BLOCKS[b][way]))
             updated = jnp.where(wide_valid[inside], residual + gain[inside] * projected, residual)
             out_ref[here, :] = updated.astype(jnp.bfloat16)
-
+            out_copy(b, way).start()
+
+    q_copy.wait()
     stack_queries()
     pl.semaphore_wait(barrier, len(peers))
     for what in FIRST_SENDS:
@@ -401,8 +411,12 @@
     for b in (0, 1):
         for d in range(NX):
             to_sibling(d, b).wait_send()
+    stream_copy.wait()
     finish(0)
     finish(1)
+    for b in (0, 1):
+        for way in (0, 1):
+            out_copy(b, way).wait()
     for b in (0, 1):
         for kind in range(3):
             for way in (0, 1):
@@ -410,15 +424,18 @@
 
 
 def local(stream_rows, picks, router, queries, keys, values, out_weight):
-    vmem = pl.BlockSpec(memory_space=pltpu.VMEM)
+    vmem, anywhere = pl.BlockSpec(memory_space=pltpu.VMEM), pl.BlockSpec(memory_space=pl.ANY)
     bf16, f32 = jnp.bfloat16, jnp.float32
     dma = pltpu.SemaphoreType.DMA
     return pl.pallas_call(
         kernel,
         out_shape=jax.ShapeDtypeStruct(stream_rows.shape, bf16),
-        in_specs=[vmem] * 6 + [pl.BlockSpec(memory_space=pl.ANY)],
-        out_specs=vmem,
+        in_specs=[anywhere] + [vmem] * 4 + [anywhere] * 2,
+        out_specs=anywhere,
         scratch_shapes=[
+            pltpu.VMEM(queries.shape, bf16),
+            pltpu.VMEM(stream_rows.shape, bf16),
+            pltpu.VMEM(stream_rows.shape, bf16),
             pltpu.VMEM((CAP, 2 * HD), bf16),
             pltpu.VMEM((sum(UNIT_ROWS), 2 * HD), bf16),
             pltpu.VMEM((GROUP * CAP, HD), bf16),
@@ -441,6 +458,8 @@
             dma((12,)),
             dma((12,)),
             dma,
+            dma((2,)),
+            dma((4,)),
         ],
         compiler_params=pltpu.CompilerParams(
             collective_id=0, has_side_effects=True, vmem_limit_bytes=56 * 2**20

time: 64.8 us -> 64.4 us (level)
  no operation moved by 1% of the time
where the time goes in v5:
time: 64.4 us; the launch traced here: 64.1 us
  Pallas kernels  62.2 us (97%)
  local copies, waits for them, and re-layouts  1.87 us (3%)
    pallas_call x1, Pallas kernels, local(): pl.pallas_call(kernel, out_shape=jax.ShapeDtypeStruct(stream_rows.shape,...  62.2 us
    unnamed x1, local copies, waits for them, and re-layouts  1.87 us

profile of v5, /device:TPU:25, one launch (start us, length us, event | category | flops | bytes accessed | tf_op | source)
XLA Modules:
  0.0 64.1 jit_solution(8940111384897447289)
XLA Ops:
  0.0 62.2 %shard_map.73 = bf16[288,896]{1,0:T(8,128)(2,1)} custom-call(bf16[288,512]{1,0:T(8,128)(2,1)} %q_hbm.1, bf16[288,128]{1,0:T(8,128)(2,1)} %k_ref.1, bf16[288,128]{1,0:T(8,128)(2,1)} %v_ref.1, s32[288]{0:T(512)} %picks_ref.1, f32[288]{0:T(512)} %router_ref.1, bf16[288,896]{1,0:T(8,128)(2,1)} %stream_hbm.1, bf16[512,7168]{1,0:T(8,128)(2,1)} %w_hbm.1), custom_call_target="tpu_custom_call" | custom-call | flops 8000000000 | bytes 10000000 | tf_op jit(solution)/shard_map/pallas_call | solution.py:430
  62.2 1.9 %copy.9 = bf16[288,896]{1,0:T(8,128)(2,1)} copy(bf16[288,896]{1,0:T(8,128)(2,1)} %shard_map.73) | data formatting | bytes 1032192

commit v6 on v5

--- a/solution.py
+++ b/solution.py
@@ -178,8 +178,35 @@
             src, place(name), send_sem.at[i], recv_sem.at[i], device_id=target, device_id_type=MESH
         )
 
+    def need(name, yy):
+        kind = name[0]
+        if kind in ("ZR", "ZL"):
+            return {0: None, 3: yy >= 1, 1: yy == 3, 2: yy >= 2}[ROW_OF[name[1]]]
+        if kind == "YB":
+            return {"P": yy >= 1, "M": yy == 3, "2": yy >= 2}[name[1]]
+        if kind == "YP":
+            return yy >= 1
+        if kind == "YM":
+            return yy == 3 if name[1] in UPWARDS else jnp.logical_or(yy == 3, yy == 0)
+        return yy >= 2
+
+    def sent(name):
+        if name[0] in ("ZR", "ZL"):
+            return need(name, y)
+        down_going = name[0] in ("YM", "YM2") or name == ("YB", "M")
+        return need(name, wrap(y - 1 if down_going else y + 1, NY))
+
+    def when(condition, action):
+        if condition is None:
+            action()
+        else:
+
+            @pl.when(condition)
+            def _():
+                action()
+
     def start(name):
-        transfer(name).start()
+        when(sent(name), transfer(name).start)
 
     def open_ring(stream):
         start(("ZR", stream, 1))
@@ -190,20 +217,24 @@
         start(("YM", offset))
 
     def arrive(name):
-        transfer(name).wait_recv()
         kind = name[0]
-        if kind in ("ZR", "ZL"):
-            _, stream, step = name
-            if step < TURNS[stream][0 if kind == "ZR" else 1]:
-                start((kind, stream, step + 1))
-            if stream == "A":
-                open_column(step if kind == "ZL" else (-step if step < 4 else 4))
-        elif kind == "YP" and name[1] in UPWARDS:
-            start(("YP2", name[1]))
-        elif kind == "YM" and name[1] not in UPWARDS:
-            start(("YM2", name[1]))
-        elif name == ("YB", "P"):
-            start(("YB", "2"))
+
+        def receive():
+            transfer(name).wait_recv()
+            if kind in ("ZR", "ZL"):
+                _, stream, step = name
+                if step < TURNS[stream][0 if kind == "ZR" else 1]:
+                    transfer((kind, stream, step + 1)).start()
+            elif kind == "YP" and name[1] in UPWARDS:
+                start(("YP2", name[1]))
+            elif kind == "YM" and name[1] not in UPWARDS:
+                start(("YM2", name[1]))
+            elif name == ("YB", "P"):
+                start(("YB", "2"))
+
+        when(need(name, y), receive)
+        if kind in ("ZR", "ZL") and name[1] == "A":
+            open_column(name[2] if kind == "ZL" else (-name[2] if name[2] < 4 else 4))
         for stream in OPENS.get(name, ()):
             open_ring(stream)
 
@@ -250,17 +281,16 @@
         def _():
             if fill:
                 block = jnp.transpose(held[here, HD:])
-                real = block < FILL / 2
+                real = jnp.abs(block) < FILL / 2
                 vt[:HD, :n] = jnp.where(real, block, 0).astype(jnp.bfloat16)
                 vt[HD:, :n] = jnp.where(real[: VROWS - HD], 1, 0).astype(jnp.bfloat16)
-            hide = [jnp.where(shown, 0.0, NEG) for shown in seen]
 
             def score(cols):
                 raw = qk(held[here, :HD], cols)
                 parts, first = [], 0
-                for name, shift in zip(UNITS[u], hide):
+                for name, shown in zip(UNITS[u], seen):
                     rows = ROWS[part_of(name)]
-                    parts.append(raw[first : first + rows] + shift)
+                    parts.append(jnp.where(shown, raw[first : first + rows], NEG))
                     first += rows
                 return jnp.concatenate(parts, axis=0)
 
@@ -407,7 +437,7 @@
     gain = jnp.sum(jnp.where(eye, router, 0.0), axis=1, keepdims=True)
     wide_valid = lax.broadcasted_iota(jnp.int32, (CAP, WIDTH), 0).astype(jnp.float32) < count
     for name in G_IDS:
-        transfer(name).wait_send()
+        when(sent(name), transfer(name).wait_send)
     for b in (0, 1):
         for d in range(NX):
             to_sibling(d, b).wait_send()

time: 64.4 us -> 63.6 us (0.988)
  Pallas kernels: 62.2 us -> 61 us
    pallas_call x1, Pallas kernels: 62.2 us -> 61 us  [local(): pl.pallas_call(kernel, out_shape=jax.ShapeDtypeStruct(stream_rows.shape,...]
where the time goes in v6:
time: 63.6 us; the launch traced here: 62.9 us
  Pallas kernels  61 us (96%)
  local copies, waits for them, and re-layouts  1.87 us (3%)
    pallas_call x1, Pallas kernels, local(): pl.pallas_call(kernel, out_shape=jax.ShapeDtypeStruct(stream_rows.shape,...  61 us
    unnamed x1, local copies, waits for them, and re-layouts  1.87 us

profile of v6, /device:TPU:25, one launch (start us, length us, event | category | flops | bytes accessed | tf_op | source)
XLA Modules:
  0.0 62.9 jit_solution(5652407678933477200)
XLA Ops:
  0.0 61.0 %shard_map.73 = bf16[288,896]{1,0:T(8,128)(2,1)} custom-call(bf16[288,512]{1,0:T(8,128)(2,1)} %q_hbm.1, bf16[288,128]{1,0:T(8,128)(2,1)} %k_ref.1, bf16[288,128]{1,0:T(8,128)(2,1)} %v_ref.1, s32[288]{0:T(512)} %picks_ref.1, f32[288]{0:T(512)} %router_ref.1, bf16[288,896]{1,0:T(8,128)(2,1)} %stream_hbm.1, bf16[512,7168]{1,0:T(8,128)(2,1)} %w_hbm.1), custom_call_target="tpu_custom_call" | custom-call | flops 8000000000 | bytes 10000000 | tf_op jit(solution)/shard_map/pallas_call | solution.py:460
  61.0 1.9 %copy.9 = bf16[288,896]{1,0:T(8,128)(2,1)} copy(bf16[288,896]{1,0:T(8,128)(2,1)} %shard_map.73) | data formatting | bytes 1032192
